TPU v7x, 512 devices: a whole 4x4x16 slice. The times are simulated.
512 devices in a mesh: dp: 16 (over z_lo, core), mp: 32 (over x, y, z_hi).
Axes of the slice: x: 4, y: 4, z: 16 (z_hi: 2, z_lo: 8; z = z_hi * 8 + z_lo), core: 2. Of those that a mesh axis runs over, the one named last changes fastest.
Arguments:
- inputs: bfloat16 [8192, 4608], P(('dp', 'mp')), may hold values from -6 to 6
- out_grad: bfloat16 [8192, 4608], P(('dp', 'mp')), may hold values from -6 to 6
- gate_pre: bfloat16 [8192, 36864], P('dp', 'mp'), may hold values from -6 to 6
- up_pre: bfloat16 [8192, 36864], P('dp', 'mp'), may hold values from -6 to 6
- hidden_grad: bfloat16 [8192, 36864], P('dp', 'mp'), may hold values from -4 to 4
- q_start: float32 [36864, 96], P('mp'), may hold values from -0.03125 to 0.03125
Outputs:
- p_factors: float32 [4608, 96], replicated
- q_factors: float32 [36864, 96], P('mp')
All inputs are finite; a program needn't handle non-finite values.
Results may differ from a plain program's by a relative error of at most 0.0003.
Values sent between devices are 32-bit elements; how exact they have to be, the bound alone decides.
A program may use at most 64 MiB of HBM per device.

v0:
```python
import math

import jax
import jax.numpy as jnp
from jax import lax
from jax.sharding import PartitionSpec as P

D = 4608


precise = lax.Precision.HIGHEST


def activations(gate_pre, up_pre, hidden_grad):
    gate = gate_pre.astype(jnp.float32)
    upper = up_pre.astype(jnp.float32)
    cotan = hidden_grad.astype(jnp.float32)
    sigmoid = 1.0 / (1.0 + jnp.exp(-gate))
    silu_value = gate * sigmoid
    hidden = silu_value * upper
    gate_grad = cotan * upper * sigmoid * (1.0 + gate * (1.0 - sigmoid))
    up_grad = cotan * silu_value
    return (gate_grad, up_grad, hidden)


def lower_inverse(lower):
    columns = lower.shape[-1]
    identity = jnp.eye(columns, dtype=jnp.float32)
    done_rows = []
    for index in range(columns):
        next_row = jnp.broadcast_to(identity[index], (lower.shape[0], columns))
        if index > 0:
            earlier = jnp.stack(done_rows, axis=1)
            next_row = next_row - jnp.einsum(
                "kj,kjc->kc", lower[:, index, :index], earlier, precision=precise
            )
        done_rows.append(next_row / lower[:, index, index : index + 1])
    return jnp.stack(done_rows, axis=1)


def gram_blocks(factor, columns):
    blocks = factor.reshape(factor.shape[0], 3, columns)
    return jnp.einsum("dkc,dke->kce", blocks, blocks, precision=precise)


def orthonormal(factor, grams, columns):
    lower = jnp.linalg.cholesky(grams)
    inverse = lower_inverse(lower)
    blocks = factor.reshape(factor.shape[0], 3, columns)
    basis = jnp.einsum("dkc,kjc->dkj", blocks, inverse, precision=precise)
    return basis.reshape(factor.shape[0], 3 * columns)


def three_products(left_one, left_two, right_blocks, columns, form):
    return jnp.concatenate(
        [
            jnp.einsum(form, left_one[0], right_blocks[:, :columns], precision=precise),
            jnp.einsum(
                form, left_one[1], right_blocks[:, columns : 2 * columns], precision=precise
            ),
            jnp.einsum(form, left_two, right_blocks[:, 2 * columns :], precision=precise),
        ],
        axis=1,
    )


def on_device(inputs, out_grad, gate_pre, up_pre, hidden_grad, q_start):
    factor_rank = q_start.shape[1] // 3
    groups = lax.axis_size("dp")
    gate_grad, up_grad, hidden = activations(gate_pre, up_pre, hidden_grad)
    mixture = lax.psum_scatter(
        three_products((gate_grad, up_grad), hidden, q_start, factor_rank, "tf,fc->tc"),
        "mp",
        scatter_dimension=0,
        tiled=True,
    )
    in_float = inputs.astype(jnp.float32)
    grad_float = out_grad.astype(jnp.float32)
    local_factor = three_products(
        (in_float, in_float), grad_float, mixture, factor_rank, "td,tc->dc"
    )
    factor = lax.psum(local_factor, ("dp", "mp")) / groups
    basis = orthonormal(factor, gram_blocks(factor, factor_rank), factor_rank)
    image = three_products((in_float, in_float), grad_float, basis, factor_rank, "td,dc->tc")
    image_all = lax.all_gather(image, "mp", axis=0, tiled=True)
    local_basis = three_products((gate_grad, up_grad), hidden, image_all, factor_rank, "tf,tc->fc")
    q_factors = lax.psum(local_basis, "dp") / groups
    return (basis * math.sqrt(D), q_factors)


def solution(mesh):
    in_specs = (
        P(("dp", "mp"), None),
        P(("dp", "mp"), None),
        P("dp", "mp"),
        P("dp", "mp"),
        P("dp", "mp"),
        P("mp", None),
    )
    out_specs = (P(), P("mp", None))
    return jax.shard_map(
        on_device, mesh=mesh, in_specs=in_specs, out_specs=out_specs, check_vma=False
    )
```

profile of v0, /device:TPU:1, one launch (start us, length us, event | category | flops | bytes accessed | tf_op | source)
XLA Modules:
  0.0 1186.7 jit_solution(2039092106204592844)
XLA Ops:
  7.3 4.7 fusion.9
  12.0 3.0 fusion.7
  15.0 1.0 fusion.1
  16.0 1.4 copy-done.1
  17.5 2.3 fusion.19
  19.7 0.8 copy.2060
  20.7 287.2 %reduce-scatter.4.cloned.1.call-done = f32[16,96]{1,0:T(8,128)} async-done(((f32[512,96]{1,0:T(8,128)}), f32[16,96]{1,0:T(8,128)}) %reduce-scatter.4.cloned.1.call-update) | async-done | bytes 6160
  307.9 1.2 convolution_bitcast_fusion.1
  309.1 1.1 convolution_bitcast_fusion.2
  310.2 1.2 convolution_bitcast_fusion
  311.4 1.3 pad_maximum_fusion
  313.7 486.8 %all-reduce.3.cloned.1.call-done = f32[4608,96]{0,1:T(8,128)} async-done(((f32[4608,96]{0,1:T(8,128)}), f32[4608,96]{0,1:T(8,128)}) %all-reduce.3.cloned.1.call-update) | async-done | bytes 1769488 | tf_op jit(solution)/shard_map/psum | solution.py:82
  800.4 1.6 broadcast_multiply_fusion.1
  802.1 1.7 fusion.122
  803.9 8.8 custom-call.4
  829.2 1.6 fusion.123
  832.1 142.9 %all_gather.3 = f32[512,96]{1,0:T(8,128)S(1)} all-gather(f32[16,96]{1,0:T(8,128)S(1)} %pad_maximum_fusion.3), channel_id=1, replica_groups=mesh['dp'=16,'mp'=32] {'mp'}, dimensions={0}, use_global_device_ids=true | all-gather | bytes 202752 | tf_op jit(solution)/shard_map/all_gather | solution.py:85
  975.0 1.5 fusion.15
  976.5 2.1 fusion.8
  978.7 2.1 fusion.6
  980.8 0.8 pad_maximum_fusion.1
  981.6 1.4 broadcast_multiply_fusion
  983.0 195.4 %all-reduce.5.cloned.1.call-done = f32[1152,96]{0,1:T(8,128)} async-done(((f32[1152,96]{0,1:T(8,128)}), f32[1152,96]{0,1:T(8,128)}) %all-reduce.5.cloned.1.call-update) | async-done | bytes 442384 | tf_op jit(solution)/shard_map/psum | solution.py:87
  1178.4 1.8 broadcast_multiply_fusion.2
  (170 shorter events, 18.4 us)
Async XLA Ops:
  7.2 300.7 %copy-start = (bf16[16,4608]{1,0:T(8,128)(2,1)S(1)}, bf16[16,4608]{1,0:T(8,128)(2,1)}, u32[]{:S(2)}) copy-start(bf16[16,4608]{1,0:T(8,128)(2,1)} %param.6) | copy-start | bytes 442372
  7.2 4.8 copy-start.6
  7.2 4.8 copy-start.11
  7.2 300.7 %reduce-scatter.4.cloned.1.call-start = ((), (), s32[]{:S(2)}) async-start(), calls=%async_computation.3 | async-start | bytes 270336
  7.2 4.8 copy-start.8
  12.0 3.0 copy-start.5
  16.0 1.4 copy-start.1
  17.5 292.7 %copy-start.10 = (bf16[16,4608]{1,0:T(8,128)(2,1)S(1)}, bf16[16,4608]{1,0:T(8,128)(2,1)}, u32[]{:S(2)}) copy-start(bf16[16,4608]{1,0:T(8,128)(2,1)} %param.7) | copy-start | bytes 442372
  20.6 779.8 %all-reduce.3.cloned.1.call-start = ((), (), s32[]{:S(2)}) async-start(), calls=%async_computation.1 | async-start | bytes 3538944 | tf_op jit(solution)/shard_map/psum | solution.py:82
  312.8 865.6 %all-reduce.5.cloned.1.call-start = ((), (), s32[]{:S(2)}) async-start(), calls=%async_computation.2 | async-start | bytes 884736 | tf_op jit(solution)/shard_map/psum | solution.py:87
  829.2 145.9 %copy-start.2 = (f32[512,1152]{1,0:T(8,128)S(1)}, f32[512,1152]{1,0:T(8,128)}, u32[]{:S(2)}) copy-start(f32[512,1152]{1,0:T(8,128)} %copy-done.1) | copy-start | bytes 7077892
  830.8 145.7 %copy-start.3 = (f32[3,32,4608]{2,1,0:T(8,128)}, f32[3,32,4608]{2,1,0:T(8,128)S(1)}, u32[]{:S(2)}) copy-start(f32[3,32,4608]{2,1,0:T(8,128)S(1)} %fusion.123) | copy-start | bytes 5308420
  831.2 145.3 %copy-start.7 = (bf16[512,1152]{1,0:T(8,128)(2,1)S(1)}, bf16[512,1152]{1,0:T(8,128)(2,1)}, u32[]{:S(2)}) copy-start(bf16[512,1152]{1,0:T(8,128)(2,1)} %param.8) | copy-start | bytes 3538948
  976.5 2.1 copy-start.9
  978.6 2.9 copy-start.4
Sparse Core Ops, SparseCore 0:
  20.7 287.0 reduce-scatter.3
  314.6 485.7 all-reduce.2
  981.7 196.6 all-reduce.4
where the time goes:
time: 1190 us
  waiting for transfers between devices  969 us (81%)
  blocking collectives  143 us (12%)
  matrix products  27.7 us (2%)
  other arithmetic  25.6 us (2%)
  between operations  14.6 us (1%)
    psum x1, waiting for transfers between devices, on_device(): factor = lax.psum(local_factor, ('dp', 'mp')) / groups  487 us
    unnamed x4, waiting for transfers between devices  287 us
    psum x1, waiting for transfers between devices, on_device(): q_factors = lax.psum(local_basis, 'dp') / groups  195 us
    all_gather x1, blocking collectives, on_device(): image_all = lax.all_gather(image, 'mp', axis=0, tiled=True)  143 us
  transfers between devices with their start and end apart: 3, of which 3 were waited for; matrix products, arithmetic and copies ran while one was open for 0% of the time, Pallas kernels for 0%

commit v1 on v0

v1 whole, which is shorter than its diff:
```python
import functools
import math

import jax
import jax.numpy as jnp
from jax import lax
from jax.experimental import pallas as pl
from jax.experimental.pallas import tpu as pltpu
from jax.sharding import PartitionSpec as P

MESH = pl.DeviceIdType.MESH
F32 = jnp.float32
BF16 = jnp.bfloat16
HIGH = lax.Precision.HIGHEST

D = 4608
TOK = 512
FFL = 1152
ROWS = 16
RANK = 32
W = 3 * RANK
LANES = 128
SIDE = 4
PLANE = SIDE * SIDE
ZLO = 8
DEPTH = 16
GROUPS = 16

PB = 224
PB_USED = 216
PS = PB // SIDE
ZROWS = 64
QB = 448
QB_USED = 432
QS = QB // ZLO


def split(value):
    high = value.astype(BF16)
    low = (value - high.astype(F32)).astype(BF16)
    return high, low


def mm(left, right):
    return lax.dot_general(
        left, right, (((1,), (0,)), ((), ())), preferred_element_type=F32
    )


def mm_t(left, right, precision=None):
    return lax.dot_general(
        left,
        right,
        (((1,), (1,)), ((), ())),
        preferred_element_type=F32,
        precision=precision,
    )


def pieces(start, count, used):
    out = []
    at = start
    while at < start + count:
        block, row = divmod(at, used)
        here = min(used - row, start + count - at)
        out.append((block, row, at - start, here))
        at += here
    return out


def kernel(
    in_ref,
    og_ref,
    gate_ref,
    up_ref,
    cot_ref,
    q_ref,
    p_out,
    q_out,
    acts,
    qs,
    mpart,
    mrecv,
    m32,
    mzrecv,
    pb,
    pcrecv,
    r1,
    s1,
    r2,
    s2,
    r3,
    s3,
    pf,
    ptf,
    xs,
    pfin,
    img,
    qb,
    qcrecv,
    qh,
    qr,
    qf,
    ms,
    mr,
    mzs,
    mzr,
    pcs,
    pcr,
    r1s,
    r1r,
    r2s,
    r2r,
    r3s,
    r3r,
    g3s,
    g3r,
    g2s,
    g2r,
    g1s,
    g1r,
    gcs,
    gcr,
    izs,
    izr,
    ixs,
    ixr,
    qcs,
    qcr,
    qrs,
    qrr,
    qgs,
    qgr,
    qds,
    qdr,
    outs,
):
    dp, mp = lax.axis_index("dp"), lax.axis_index("mp")
    core, zl = lax.rem(dp, 2), lax.div(dp, 2)
    zh, plane = lax.rem(mp, 2), lax.div(mp, 2)
    xx, yy = lax.div(plane, SIDE), lax.rem(plane, SIDE)
    z = zh * ZLO + zl
    sibling = (zl * 2 + 1 - core, mp)
    opposite = (dp, plane * 2 + 1 - zh)

    def plane_peer(index):
        return (dp, index * 2 + zh)

    def z_peer(index):
        return (lax.rem(index, ZLO) * 2 + core, plane * 2 + lax.div(index, ZLO))

    def side_peer(axis, index):
        along_x = (dp, (index * SIDE + yy) * 2 + zh)
        along_y = (dp, (xx * SIDE + index) * 2 + zh)
        return along_x if axis == 0 else along_y

    def side(axis):
        return xx if axis == 0 else yy

    def remote(src, dst, send, recv, to):
        return pltpu.make_async_remote_copy(
            src_ref=src,
            dst_ref=dst,
            send_sem=send,
            recv_sem=recv,
            device_id=to,
            device_id_type=MESH,
        )

    def around(count, body):
        def step(index, carry):
            body(index)
            return carry

        lax.fori_loop(1, count, step, 0)

    barrier = pltpu.get_barrier_semaphore()

    def greet(d):
        pl.semaphore_signal(
            barrier,
            inc=1,
            device_id=plane_peer(lax.rem(plane + d, PLANE)),
            device_id_type=MESH,
        )
        pl.semaphore_signal(
            barrier,
            inc=1,
            device_id=z_peer(lax.rem(z + d, DEPTH)),
            device_id_type=MESH,
        )

    around(DEPTH, greet)
    pl.semaphore_signal(barrier, inc=1, device_id=sibling, device_id_type=MESH)

    def activate(i, carry):
        rows = pl.ds(pl.multiple_of(i * 16, 16), 16)
        low_rows = pl.ds(pl.multiple_of(TOK + i * 16, 16), 16)
        g = gate_ref[rows, :].astype(F32)
        u = up_ref[rows, :].astype(F32)
        e = cot_ref[rows, :].astype(F32)
        s = 1.0 / (1.0 + jnp.exp(-g))
        silu = g * s
        values = (e * u * s * (1.0 + g * (1.0 - s)), e * silu, silu * u)
        for k, value in enumerate(values):
            high, low = split(value)
            acts[k, rows, :] = high
            acts[k, low_rows, :] = low
        return carry

    lax.fori_loop(0, TOK // 16, activate, 0)

    q_high, q_low = split(q_ref[...])
    qs[...] = jnp.zeros_like(qs)
    qs[:, 0:W] = q_high
    qs[:, LANES : LANES + W] = q_low

    lane = lax.broadcasted_iota(jnp.int32, (TOK, LANES), 1)
    for k in range(3):
        first = mm(acts[k, 0:TOK, :], qs[...])
        second = mm(acts[k, TOK : 2 * TOK, :], qs[:, 0:LANES])
        both = first[:, 0:LANES] + first[:, LANES:] + second
        if k == 0:
            mpart[...] = both
        else:
            mpart[...] = jnp.where(lane >= k * RANK, both, mpart[...])

    pl.semaphore_wait(barrier, 2 * (DEPTH - 1) + 1)

    def m_copy(d):
        to = lax.rem(plane + d, PLANE)
        return remote(
            mpart.at[pl.ds(pl.multiple_of(to * 32, 32), 32)],
            mrecv.at[d - 1],
            ms.at[d - 1],
            mr.at[d - 1],
            plane_peer(to),
        )

    around(PLANE, lambda d: m_copy(d).start())
    around(PLANE, lambda d: m_copy(d).wait_recv())
    m32[...] = mpart[pl.ds(pl.multiple_of(plane * 32, 32), 32), :] + jnp.sum(
        mrecv[...], axis=0
    )
    mz_copy = remote(
        m32.at[pl.ds(pl.multiple_of((1 - zh) * 16, 16), 16)],
        mzrecv,
        mzs.at[0],
        mzr.at[0],
        opposite,
    )
    mz_copy.start()
    mz_copy.wait_recv()
    mixture = m32[pl.ds(pl.multiple_of(zh * 16, 16), 16), :] + mzrecv[...]
    m_high, m_low = split(mixture * (1.0 / GROUPS))
    m_both = jnp.concatenate([m_high.astype(F32), m_low.astype(F32)], axis=0)
    m_turned = m_both.T.astype(BF16)

    def p_blocks(half, portion):
        columns = pl.ds(
            pl.multiple_of((half * 2 + portion) * (9 * LANES), LANES), 9 * LANES
        )
        b_in = in_ref[:, columns]
        b_out = og_ref[:, columns]
        top = mm(m_turned[0 : 2 * RANK], jnp.concatenate([b_in, b_in], axis=0))
        low = mm(m_turned[2 * RANK : W], jnp.concatenate([b_out, b_out], axis=0))
        base = (half * 2 + portion) * SIDE
        for tile in range(9):
            at = slice(tile * LANES, (tile + 1) * LANES)
            for part, start in ((top[:, at], 0), (low[:, at], 2 * RANK)):
                for block, row, first, count in pieces(
                    tile * W + start, part.shape[0], PB_USED
                ):
                    pb[base + block, row : row + count, :] = part[first : first + count]
        for block in range(SIDE):
            pb[base + block, PB_USED:PB, :] = jnp.zeros((PB - PB_USED, LANES), F32)

    def pc_copy(index):
        return remote(
            pb.at[(1 - core) * 8 + index],
            pcrecv.at[index],
            pcs.at[index],
            pcr.at[index],
            sibling,
        )

    for portion in range(2):
        p_blocks(1 - core, portion)
        for f in range(SIDE):
            pc_copy(portion * SIDE + f).start()
    for portion in range(2):
        p_blocks(core, portion)

    def r1_copy(portion, d):
        to = lax.rem(side(portion) + d, SIDE)
        index = portion * SIDE + to
        at = portion * 3 + d - 1
        return remote(
            pb.at[core * 8 + index],
            r1.at[at],
            r1s.at[at],
            r1r.at[at],
            side_peer(portion, to),
        )

    for d in (2, 1, 3, 0):
        for portion in range(2):
            index = portion * SIDE + lax.rem(side(portion) + d, SIDE)
            pc_copy(index).wait_recv()
            pb[core * 8 + index] = pb[core * 8 + index] + pcrecv[index]
            if d:
                r1_copy(portion, d).start()

    def r2_copy(portion, d):
        axis = 1 - portion
        to = lax.rem(side(axis) + d, SIDE)
        at = portion * 3 + d - 1
        return remote(
            s1.at[portion, pl.ds(pl.multiple_of(to * PS, 8), PS)],
            r2.at[at],
            r2s.at[at],
            r2r.at[at],
            side_peer(axis, to),
        )

    for portion in range(2):
        for d in (1, 3, 2):
            r1_copy(portion, d).wait_recv()
        s1[portion] = (
            pb[core * 8 + portion * SIDE + side(portion)]
            + r1[portion * 3]
            + r1[portion * 3 + 1]
            + r1[portion * 3 + 2]
        )
        for d in (2, 1, 3):
            r2_copy(portion, d).start()
    for portion in range(2):
        for d in (1, 3, 2):
            r2_copy(portion, d).wait_recv()
        own = pl.ds(pl.multiple_of(side(1 - portion) * PS, 8), PS)
        s2[portion * ZROWS : portion * ZROWS + PS, :] = (
            s1[portion, own, :]
            + r2[portion * 3]
            + r2[portion * 3 + 1]
            + r2[portion * 3 + 2]
        )
        s2[portion * ZROWS + PS : (portion + 1) * ZROWS, :] = jnp.zeros(
            (ZROWS - PS, LANES), F32
        )

    def r3_copy(d):
        to = lax.rem(z + d, DEPTH)
        return remote(
            s2.at[pl.ds(pl.multiple_of(to * 8, 8), 8)],
            r3.at[d - 1],
            r3s.at[d - 1],
            r3r.at[d - 1],
            z_peer(to),
        )

    around(DEPTH, lambda d: r3_copy(d).start())
    around(DEPTH, lambda d: r3_copy(d).wait_recv())
    z_own = pl.ds(pl.multiple_of(z * 8, 8), 8)
    s3[z_own, :] = s2[z_own, :] + jnp.sum(r3[...], axis=0)

    def g3_copy(d):
        return remote(
            s3.at[z_own],
            s3.at[z_own],
            g3s.at[d - 1],
            g3r.at[d - 1],
            z_peer(lax.rem(z + d, DEPTH)),
        )

    around(DEPTH, lambda d: g3_copy(d).start())
    around(DEPTH, lambda d: g3_copy(d).wait_recv())

    def own_block(portion):
        return (core * 2 + portion) * SIDE + side(portion)

    def g2_copy(portion, d):
        axis = 1 - portion
        at = portion * 3 + d - 1
        rows = pl.ds(pl.multiple_of(side(axis) * PS, 8), PS)
        return remote(
            pf.at[own_block(portion), rows],
            pf.at[own_block(portion), rows],
            g2s.at[at],
            g2r.at[at],
            side_peer(axis, lax.rem(side(axis) + d, SIDE)),
        )

    for portion in range(2):
        rows = pl.ds(pl.multiple_of(side(1 - portion) * PS, 8), PS)
        pf[own_block(portion), rows, :] = s3[
            portion * ZROWS : portion * ZROWS + PS, :
        ]
        for d in (2, 1, 3):
            g2_copy(portion, d).start()

    def g1_copy(portion, d):
        at = portion * 3 + d - 1
        return remote(
            pf.at[own_block(portion)],
            pf.at[own_block(portion)],
            g1s.at[at],
            g1r.at[at],
            side_peer(portion, lax.rem(side(portion) + d, SIDE)),
        )

    def gc_copy(portion, d):
        f = lax.rem(side(portion) + SIDE - d, SIDE)
        index = portion * SIDE + f
        block = core * 8 + index
        return remote(
            pf.at[block], pf.at[block], gcs.at[index], gcr.at[index], sibling
        )

    for portion in range(2):
        for d in (1, 3, 2):
            g2_copy(portion, d).wait_recv()
        for d in (2, 1, 3):
            g1_copy(portion, d).start()
        gc_copy(portion, 0).start()
    for d in (1, 3, 2):
        for portion in range(2):
            g1_copy(portion, d).wait_recv()
            gc_copy(portion, d).start()
    for d in range(SIDE):
        for portion in range(2):
            gc_copy(portion, d).wait_recv()

    for tile in range(D // LANES):
        at = slice(tile * LANES, (tile + 1) * LANES)
        parts = [
            pf[block, row : row + count, :]
            for block, row, _, count in pieces(tile * W, W, PB_USED)
        ]
        whole = parts[0] if len(parts) == 1 else jnp.concatenate(parts, axis=0)
        ptf[:, at] = whole
        high, low = split(whole)
        xs[0:W, at] = high
        xs[LANES : LANES + W, at] = low
    xs[W:LANES, :] = jnp.zeros((LANES - W, D), BF16)
    xs[LANES + W : LANES + W + ROWS, :] = in_ref[...]
    xs[LANES + W + ROWS :, :] = og_ref[...]
    products = mm_t(xs[...], xs[...])
    near, far = products[:, 0:LANES], products[:, LANES:]
    gram = near[0:LANES] + near[LANES:] + far[0:LANES] + far[LANES:]
    onto = near[LANES + W :] + far[LANES + W :]

    row_at = lax.broadcasted_iota(jnp.int32, (RANK, LANES), 0)
    lane_at = lax.broadcasted_iota(jnp.int32, (RANK, LANES), 1)
    inverse = []
    left = [gram[k * RANK : (k + 1) * RANK] for k in range(3)]
    right = [(lane_at == row_at + k * RANK).astype(F32) for k in range(3)]
    for j in range(RANK - 1):
        for k in range(3):
            at = k * RANK + j
            pivot = left[k][j : j + 1, at : at + 1]
            column = left[k][:, at : at + 1] / pivot
            factor = jnp.where(row_at > j, column, 0.0)
            left[k] = left[k] - factor * left[k][j : j + 1, :]
            right[k] = right[k] - factor * right[k][j : j + 1, :]
    for k in range(3):
        diagonal = jnp.sum(
            jnp.where(lane_at == row_at + k * RANK, left[k], 0.0), axis=1, keepdims=True
        )
        inverse.append(right[k] / jnp.sqrt(diagonal))
    inverse.append(jnp.zeros((RANK, LANES), F32))
    inverse = jnp.concatenate(inverse, axis=0)

    token_lane = lax.broadcasted_iota(jnp.int32, (ROWS, LANES), 1)
    onto = jnp.where(
        token_lane < 2 * RANK,
        onto[0:ROWS],
        jnp.where(token_lane < W, onto[ROWS:], 0.0),
    )
    image = mm_t(onto, inverse, HIGH) * (1.0 / GROUPS)

    img_own = pl.ds(pl.multiple_of(plane * 32 + zh * 16, 16), 16)
    img[img_own, :] = image
    iz_copy = remote(img.at[img_own], img.at[img_own], izs.at[0], izr.at[0], opposite)
    iz_copy.start()
    iz_copy.wait_recv()
    img_pair = pl.ds(pl.multiple_of(plane * 32, 32), 32)

    def ix_copy(d):
        return remote(
            img.at[img_pair],
            img.at[img_pair],
            ixs.at[d - 1],
            ixr.at[d - 1],
            plane_peer(lax.rem(plane + d, PLANE)),
        )

    around(PLANE, lambda d: ix_copy(d).start())

    def left_factor(tile, carry):
        at = pl.ds(pl.multiple_of(tile * LANES, LANES), LANES)
        turned = ptf[:, at].T
        pfin[at, :] = mm_t(turned, inverse[0:W, 0:W] * math.sqrt(D), HIGH)
        return carry

    lax.fori_loop(0, D // LANES, left_factor, 0)
    out_copy = pltpu.make_async_copy(pfin, p_out, outs.at[0])
    out_copy.start()

    around(PLANE, lambda d: ix_copy(d).wait_recv())

    img_high, img_low = split(img[...].T)
    for half in range(2):
        qb[half, QB_USED:QB, :] = jnp.zeros((QB - QB_USED, LANES), F32)
    for k in range(3):
        rows = slice(k * RANK, (k + 1) * RANK)
        both = jnp.concatenate([img_high[rows], img_low[rows]], axis=0)
        first = mm(both, acts[k, 0:TOK, :])
        second = mm(img_high[rows], acts[k, TOK : 2 * TOK, :])
        share = first[0:RANK] + first[RANK:] + second
        for tile in range(FFL // LANES):
            part = share[:, tile * LANES : (tile + 1) * LANES]
            for half, row, start, count in pieces(
                tile * W + k * RANK, RANK, QB_USED
            ):
                qb[half, row : row + count, :] = part[start : start + count]

    qc_copy = remote(qb.at[1 - core], qcrecv, qcs.at[0], qcr.at[0], sibling)
    qc_copy.start()
    qc_copy.wait_recv()
    qh[...] = qb[core] + qcrecv[...]

    def zl_peer(index):
        return (index * 2 + core, mp)

    def qr_copy(d):
        to = lax.rem(zl + d, ZLO)
        return remote(
            qh.at[pl.ds(pl.multiple_of(to * QS, 8), QS)],
            qr.at[d - 1],
            qrs.at[d - 1],
            qrr.at[d - 1],
            zl_peer(to),
        )

    around(ZLO, lambda d: qr_copy(d).start())
    around(ZLO, lambda d: qr_copy(d).wait_recv())
    q_own = pl.ds(pl.multiple_of(zl * QS, 8), QS)
    qf[core, q_own, :] = qh[q_own, :] + jnp.sum(qr[...], axis=0)

    def qg_copy(d):
        return remote(
            qf.at[core, q_own],
            qf.at[core, q_own],
            qgs.at[d - 1],
            qgr.at[d - 1],
            zl_peer(lax.rem(zl + d, ZLO)),
        )

    def qd_copy(d):
        rows = pl.ds(pl.multiple_of(lax.rem(zl + ZLO - d, ZLO) * QS, 8), QS)
        return remote(
            qf.at[core, rows], qf.at[core, rows], qds.at[d], qdr.at[d], sibling
        )

    around(ZLO, lambda d: qg_copy(d).start())
    qd_copy(0).start()

    def hand_on(d):
        qg_copy(d).wait_recv()
        qd_copy(d).start()

    around(ZLO, hand_on)
    qd_copy(0).wait_recv()
    around(ZLO, lambda d: qd_copy(d).wait_recv())

    for tile in range(FFL // LANES):
        parts = [
            qf[half, row : row + count, :]
            for half, row, _, count in pieces(tile * W, W, QB_USED)
        ]
        whole = parts[0] if len(parts) == 1 else jnp.concatenate(parts, axis=0)
        q_out[tile * LANES : (tile + 1) * LANES, :] = whole.T

    around(PLANE, lambda d: m_copy(d).wait_send())
    mz_copy.wait_send()
    for index in range(8):
        pc_copy(index).wait_send()
    for portion in range(2):
        for d in (1, 2, 3):
            r1_copy(portion, d).wait_send()
            r2_copy(portion, d).wait_send()
            g2_copy(portion, d).wait_send()
            g1_copy(portion, d).wait_send()
        for d in range(SIDE):
            gc_copy(portion, d).wait_send()
    around(DEPTH, lambda d: r3_copy(d).wait_send())
    around(DEPTH, lambda d: g3_copy(d).wait_send())
    iz_copy.wait_send()
    around(PLANE, lambda d: ix_copy(d).wait_send())
    qc_copy.wait_send()
    around(ZLO, lambda d: qr_copy(d).wait_send())
    around(ZLO, lambda d: qg_copy(d).wait_send())
    qd_copy(0).wait_send()
    around(ZLO, lambda d: qd_copy(d).wait_send())
    out_copy.wait()


def on_device(inputs, out_grad, gate_pre, up_pre, hidden_grad, q_start):
    vmem = pl.BlockSpec(memory_space=pltpu.VMEM)
    buffers = [
        pltpu.VMEM((3, 2 * TOK, FFL), BF16),
        pltpu.VMEM((FFL, 2 * LANES), BF16),
        pltpu.VMEM((TOK, LANES), F32),
        pltpu.VMEM((PLANE - 1, 32, LANES), F32),
        pltpu.VMEM((32, LANES), F32),
        pltpu.VMEM((16, LANES), F32),
        pltpu.VMEM((16, PB, LANES), F32),
        pltpu.VMEM((8, PB, LANES), F32),
        pltpu.VMEM((6, PB, LANES), F32),
        pltpu.VMEM((2, PB, LANES), F32),
        pltpu.VMEM((6, PS, LANES), F32),
        pltpu.VMEM((2 * ZROWS, LANES), F32),
        pltpu.VMEM((DEPTH - 1, 8, LANES), F32),
        pltpu.VMEM((2 * ZROWS, LANES), F32),
        pltpu.VMEM((16, PB, LANES), F32),
        pltpu.VMEM((W, D), F32),
        pltpu.VMEM((2 * LANES, D), BF16),
        pltpu.VMEM((D, W), F32),
        pltpu.VMEM((TOK, LANES), F32),
        pltpu.VMEM((2, QB, LANES), F32),
        pltpu.VMEM((QB, LANES), F32),
        pltpu.VMEM((QB, LANES), F32),
        pltpu.VMEM((ZLO - 1, QS, LANES), F32),
        pltpu.VMEM((2, QB, LANES), F32),
    ]
    counts = [15, 15, 1, 1, 8, 8, 6, 6, 6, 6, 15, 15, 15, 15, 6, 6, 6, 6, 8, 8]
    counts += [1, 1, 15, 15, 1, 1, 7, 7, 7, 7, 8, 8, 1]
    flags = [pltpu.SemaphoreType.DMA((count,)) for count in counts]
    return pl.pallas_call(
        kernel,
        out_shape=(
            jax.ShapeDtypeStruct((D, W), F32),
            jax.ShapeDtypeStruct((FFL, W), F32),
        ),
        in_specs=[vmem] * 6,
        out_specs=(pl.BlockSpec(memory_space=pl.ANY), vmem),
        scratch_shapes=buffers + flags,
        compiler_params=pltpu.CompilerParams(
            collective_id=0, has_side_effects=True, vmem_limit_bytes=56 * 2**20
        ),
        name="power_step",
    )(inputs, out_grad, gate_pre, up_pre, hidden_grad, q_start)


def solution(mesh):
    in_specs = (
        P(("dp", "mp"), None),
        P(("dp", "mp"), None),
        P("dp", "mp"),
        P("dp", "mp"),
        P("dp", "mp"),
        P("mp", None),
    )
    out_specs = (P(), P("mp", None))
    return jax.shard_map(
        on_device, mesh=mesh, in_specs=in_specs, out_specs=out_specs, check_vma=False
    )
```

time: 1190 us -> 133 us (0.11)
  waiting for transfers between devices: 969 us -> 0 us
  blocking collectives: 143 us -> 0 us
  Pallas kernels: 0 us -> 126 us
  matrix products: 27.7 us -> 0 us
  other arithmetic: 25.6 us -> 0 us
  between operations: 14.6 us -> 0.65 us
    psum x2 -> x0, waiting for transfers between devices: 682 us -> none  [the longest x1 487 us: on_device(): factor = lax.psum(local_factor, ('dp', 'mp')) / groups]
    unnamed x4 -> x0, waiting for transfers between devices: 287 us -> none
    all_gather x1 -> x0, blocking collectives: 143 us -> none  [on_device(): image_all = lax.all_gather(image, 'mp', axis=0, tiled=True)]
    pallas_call x0 -> x1, Pallas kernels: none -> 126 us  [on_device(): pl.pallas_call(kernel, out_shape=(jax.ShapeDtypeStruct((D, W), F32), jax....]
    dot_general x44 -> x0, matrix products: 27.7 us -> none  [the longest x4 8.42 us: three_products(): jnp.einsum(form, left_two, right_blocks[:, 2 * columns:], precision=precise)]
    another operation x34 -> x0, other arithmetic: 17.3 us -> none  [the longest x3 8.95 us: orthonormal(): lower = jnp.linalg.cholesky(grams)]
  transfers between devices with their start and end apart: 3 -> 0, of which waited for: 3 -> 0; matrix products, arithmetic and copies ran while one was open for 0% -> 0% of each run, Pallas kernels for 0% -> 0%
where the time goes in v1:
time: 133 us
  Pallas kernels  126 us (95%)
  local copies, waits for them, and re-layouts  6.04 us (5%)
    pallas_call x1, Pallas kernels, on_device(): pl.pallas_call(kernel, out_shape=(jax.ShapeDtypeStruct((D, W), F32), jax....  126 us
    pallas_call x2, local copies, waits for them, and re-layouts, on_device(): pl.pallas_call(kernel, out_shape=(jax.ShapeDtypeStruct((D, W), F32), jax....  3.97 us

profile of v1, /device:TPU:1, one launch (start us, length us, event | category | flops | bytes accessed | tf_op | source)
XLA Modules:
  0.0 132.9 jit_solution(11643981633906141214)
XLA Ops:
  0.6 2.1 %copy.8.q_ref = f32[1152,96]{1,0:T(8,128)} copy(f32[1152,96]{0,1:T(8,128)} %param.11) | data formatting | bytes 884736 | tf_op args[5]
  2.7 126.2 %power_step.1 = (f32[4608,96]{1,0:T(8,128)}, f32[1152,96]{1,0:T(8,128)}) custom-call(bf16[16,4608]{1,0:T(8,128)(2,1)} %in_ref.1, bf16[16,4608]{1,0:T(8,128)(2,1)} %og_ref.1, bf16[512,1152]{1,0:T(8,128)(2,1)} %gate_ref.1, bf16[512,1152]{1,0:T(8,128)(2,1)} %up_ref.1, bf16[512,1152]{1,0:T(8,128)(2,1)} %cot_ref.1, f32[1152,96]{1,0:T(8,128)} %copy.8.q_ref), custom_call_target="tpu_custom_call" | custom-call | tf_op jit(solution)/shard_map/power_step/pallas_call | solution.py:639
  128.9 0.0 copy-start
  128.9 3.0 %copy.9 = f32[4608,96]{0,1:T(8,128)} copy(f32[4608,96]{1,0:T(8,128)} %get-tuple-element.2) | data formatting | bytes 3538944 | tf_op jit(solution)/shard_map/power_step/pallas_call | solution.py:639
  131.9 0.0 copy-done
  131.9 1.0 copy.10
Async XLA Ops:
  128.9 3.0 %copy-start = (f32[1152,96]{1,0:T(8,128)S(1)}, f32[1152,96]{1,0:T(8,128)}, u32[]{:S(2)}) copy-start(f32[1152,96]{1,0:T(8,128)} %get-tuple-element.3) | copy-start | bytes 1327108

commit v2 on v1

v2 whole, which is shorter than its diff:
```python
import functools
import math

import jax
import jax.numpy as jnp
from jax import lax
from jax.experimental import pallas as pl
from jax.experimental.pallas import tpu as pltpu
from jax.sharding import PartitionSpec as P

MESH = pl.DeviceIdType.MESH
F32 = jnp.float32
BF16 = jnp.bfloat16
HIGH = lax.Precision.HIGHEST

D = 4608
TOK = 512
FFL = 1152
ROWS = 16
RANK = 32
W = 3 * RANK
LANES = 128
SIDE = 4
PLANE = SIDE * SIDE
ZLO = 8
DEPTH = 16
GROUPS = 16

TILES = D // LANES
NEAR = 2 * PLANE
SHARE = 128
QB = 448
QB_USED = 432
QS = QB // ZLO


def split(value):
    high = value.astype(BF16)
    low = (value - high.astype(F32)).astype(BF16)
    return high, low


def mm(left, right, precision=None):
    return lax.dot_general(
        left,
        right,
        (((1,), (0,)), ((), ())),
        preferred_element_type=F32,
        precision=precision,
    )


def mm_t(left, right, precision=None):
    return lax.dot_general(
        left,
        right,
        (((1,), (1,)), ((), ())),
        preferred_element_type=F32,
        precision=precision,
    )


def tiles_of(core, plane):
    x, y = divmod(plane, SIDE)
    if x == y:
        first = 12 + 6 * x + 3 * core
        return (
            [(1, first + i) for i in range(3)],
            [(32 * i, 2, first + i) for i in range(3)],
        )
    at = plane - plane // (SIDE + 1) - 1
    if core == 0:
        return (
            [(0, 3 * at), (0, 3 * at + 1)],
            [
                (0, 0, 3 * at),
                (32, 1, 3 * at),
                (64, 0, 3 * at + 1),
                (96, 1, 3 * at + 1),
            ],
        )
    return (
        [(0, 3 * at + 2), (1, at)],
        [(0, 0, 3 * at + 2), (32, 1, 3 * at + 2), (64, 2, at)],
    )


def staged(core, plane):
    x, y = lax.div(plane, SIDE), lax.rem(plane, SIDE)
    at = plane - lax.div(plane, SIDE + 1) - 1
    return jnp.where(x == y, 48 + 6 * x + 3 * core, 4 * at + 2 * core)


def pieces(start, count, used):
    out = []
    at = start
    while at < start + count:
        block, row = divmod(at, used)
        here = min(used - row, start + count - at)
        out.append((block, row, at - start, here))
        at += here
    return out


def kernel(
    in_ref,
    og_ref,
    gate_ref,
    up_ref,
    cot_ref,
    q_ref,
    p_out,
    q_out,
    gate_in,
    up_in,
    cot_in,
    acts,
    qs,
    mpart,
    mrecv,
    m32,
    mzrecv,
    bst,
    bt,
    bs,
    mall,
    yb,
    s2,
    r3,
    s3,
    zb,
    zs,
    ub,
    urecv,
    gmine,
    gsib,
    gall,
    ghalf,
    pf,
    ptf,
    pfin,
    img,
    qb,
    qcrecv,
    qh,
    qr,
    qf,
    loads,
    ms,
    mr,
    mzs,
    mzr,
    bsend,
    brecv,
    mas,
    mar,
    r3s,
    r3r,
    g3s,
    g3r,
    us,
    ur,
    gss,
    gsr,
    gps,
    gpr,
    ghs,
    ghr,
    g2s,
    g2r,
    g1s,
    g1r,
    gcs,
    gcr,
    izs,
    izr,
    ixs,
    ixr,
    qcs,
    qcr,
    qrs,
    qrr,
    qgs,
    qgr,
    qds,
    qdr,
    outs,
):
    dp, mp = lax.axis_index("dp"), lax.axis_index("mp")
    core, zl = lax.rem(dp, 2), lax.div(dp, 2)
    zh, plane = lax.rem(mp, 2), lax.div(mp, 2)
    xx, yy = lax.div(plane, SIDE), lax.rem(plane, SIDE)
    z = zh * ZLO + zl
    on_diagonal = xx == yy
    sibling = (zl * 2 + 1 - core, mp)
    opposite = (dp, plane * 2 + 1 - zh)

    def plane_peer(index):
        return (dp, index * 2 + zh)

    def z_peer(index):
        return (lax.rem(index, ZLO) * 2 + core, plane * 2 + lax.div(index, ZLO))

    def side_peer(axis, index):
        along_x = (dp, (index * SIDE + yy) * 2 + zh)
        along_y = (dp, (xx * SIDE + index) * 2 + zh)
        return along_x if axis == 0 else along_y

    def side(axis):
        return xx if axis == 0 else yy

    def after(e):
        return (
            lax.rem(core + lax.div(e, PLANE), 2),
            lax.rem(plane + lax.rem(e, PLANE), PLANE),
        )

    def before(e):
        return (
            lax.rem(core + lax.div(e, PLANE), 2),
            lax.rem(plane + PLANE - lax.rem(e, PLANE), PLANE),
        )

    def near_peer(place):
        return (zl * 2 + place[0], place[1] * 2 + zh)

    def remote(src, dst, send, recv, to):
        return pltpu.make_async_remote_copy(
            src_ref=src,
            dst_ref=dst,
            send_sem=send,
            recv_sem=recv,
            device_id=to,
            device_id_type=MESH,
        )

    def around(count, body):
        def step(index, carry):
            body(index)
            return carry

        lax.fori_loop(1, count, step, 0)

    pending = []

    def send(make, count):
        around(count, lambda d: make(d).start())
        pending.append(lambda: around(count, lambda d: make(d).wait_send()))

    def send_one(copy):
        copy.start()
        pending.append(copy.wait_send)

    def receive(make, count):
        around(count, lambda d: make(d).wait_recv())

    def finish():
        for wait in pending:
            wait()

    barrier = pltpu.get_barrier_semaphore()

    def greet(to):
        pl.semaphore_signal(barrier, inc=1, device_id=to, device_id_type=MESH)

    around(DEPTH, lambda d: greet(z_peer(lax.rem(z + d, DEPTH))))
    around(NEAR, lambda e: greet(near_peer(after(e))))

    quarter = TOK // 4

    def load(part, which):
        rows = pl.ds(part * quarter, quarter)
        src, dst = (
            (gate_ref, gate_in),
            (up_ref, up_in),
            (cot_ref, cot_in),
        )[which]
        return pltpu.make_async_copy(
            src.at[rows], dst.at[rows], loads.at[part * 3 + which]
        )

    for part in range(4):
        for which in range(3):
            load(part, which).start()

    place = 0
    for chip_type in (False, True):
        for chip in range(PLANE):
            if (chip // SIDE == chip % SIDE) != chip_type:
                continue
            for of_core in range(2):
                for array, tile in tiles_of(of_core, chip)[0]:
                    source = (in_ref, og_ref)[array]
                    bst[place] = source[:, tile * LANES : (tile + 1) * LANES].astype(F32)
                    place += 1

    def activate(i, carry):
        rows = pl.ds(pl.multiple_of(i * 16, 16), 16)
        low_rows = pl.ds(pl.multiple_of(TOK + i * 16, 16), 16)
        g = gate_in[rows, :].astype(F32)
        u = up_in[rows, :].astype(F32)
        e = cot_in[rows, :].astype(F32)
        s = 1.0 / (1.0 + jnp.exp(-g))
        silu = g * s
        values = (e * u * s * (1.0 + g * (1.0 - s)), e * silu, silu * u)
        for k, value in enumerate(values):
            high, low = split(value)
            acts[k, rows, :] = high
            acts[k, low_rows, :] = low
        return carry

    def b_copy(e, count):
        to = after(e)
        return remote(
            bst.at[pl.ds(staged(*to), count)],
            bt.at[e, pl.ds(0, count)],
            bsend.at[e - 1],
            brecv.at[e - 1],
            near_peer(to),
        )

    def b_each(e, act, diagonal):
        @pl.when(diagonal)
        def _():
            act(b_copy(e, 3))

        @pl.when(jnp.logical_not(diagonal))
        def _():
            act(b_copy(e, 2))

    def to_diagonal(e):
        chip = after(e)[1]
        return lax.div(chip, SIDE) == lax.rem(chip, SIDE)

    steps = quarter // 16
    for part in range(4):
        for which in range(3):
            load(part, which).wait()
        lax.fori_loop(part * steps, (part + 1) * steps, activate, 0)
        if part == 1:
            pl.semaphore_wait(barrier, DEPTH - 1 + NEAR - 1)
            around(NEAR, lambda e: b_each(e, lambda c: c.start(), to_diagonal(e)))
            pending.append(
                lambda: around(
                    NEAR, lambda e: b_each(e, lambda c: c.wait_send(), to_diagonal(e))
                )
            )

    q_high, q_low = split(q_ref[...])
    qs[...] = jnp.zeros_like(qs)
    qs[0:W, :] = q_high
    qs[LANES : LANES + W, :] = q_low

    lane = lax.broadcasted_iota(jnp.int32, (TOK, LANES), 1)
    for k in range(3):
        first = mm_t(acts[k, 0:TOK, :], qs[...])
        second = mm_t(acts[k, TOK : 2 * TOK, :], qs[0:LANES, :])
        both = first[:, 0:LANES] + first[:, LANES:] + second
        if k == 0:
            mpart[...] = both
        else:
            mpart[...] = jnp.where(lane >= k * RANK, both, mpart[...])

    def m_copy(d):
        to = lax.rem(plane + d, PLANE)
        return remote(
            mpart.at[pl.ds(pl.multiple_of(to * 32, 32), 32)],
            mrecv.at[d - 1],
            ms.at[d - 1],
            mr.at[d - 1],
            plane_peer(to),
        )

    send(m_copy, PLANE)
    receive(m_copy, PLANE)
    m32[...] = mpart[pl.ds(pl.multiple_of(plane * 32, 32), 32), :] + jnp.sum(
        mrecv[...], axis=0
    )
    mz_copy = remote(
        m32.at[pl.ds(pl.multiple_of((1 - zh) * 16, 16), 16)],
        mzrecv,
        mzs.at[0],
        mzr.at[0],
        opposite,
    )
    send_one(mz_copy)
    mz_copy.wait_recv()
    mixture = m32[pl.ds(pl.multiple_of(zh * 16, 16), 16), :] + mzrecv[...]
    mall[0] = mixture * (1.0 / GROUPS)

    def ma_copy(e):
        return remote(
            mall.at[0], mall.at[e], mas.at[e - 1], mar.at[e - 1], near_peer(after(e))
        )

    send(ma_copy, NEAR)

    own_tiles = staged(core, plane)
    for tile in range(2):
        bt[0, tile] = bst[own_tiles + tile]

    @pl.when(on_diagonal)
    def _():
        bt[0, 2] = bst[own_tiles + 2]

    around(NEAR, lambda e: b_each(e, lambda c: c.wait_recv(), on_diagonal))

    def round_rows(e, carry):
        rows = pl.ds(pl.multiple_of(e * ROWS, ROWS), ROWS)
        for tile in range(2):
            bs[rows, tile * LANES : (tile + 1) * LANES] = bt[e, tile].astype(BF16)

        @pl.when(on_diagonal)
        def _():
            bs[rows, 2 * LANES :] = bt[e, 2].astype(BF16)

        @pl.when(jnp.logical_not(on_diagonal))
        def _():
            bs[rows, 2 * LANES :] = jnp.zeros((ROWS, LANES), BF16)

        return carry

    lax.fori_loop(0, NEAR, round_rows, 0)
    receive(ma_copy, NEAR)

    m_turned = mall[...].reshape(NEAR * ROWS, LANES).T
    m_high, m_low = split(m_turned[0:W])
    both = mm(jnp.concatenate([m_high, m_low], axis=0), bs[...])
    yb[...] = both[0:W] + both[W:]
    middle = slice(LANES, 2 * LANES)
    nothing = jnp.zeros((RANK, LANES), F32)
    first_core = jnp.logical_and(jnp.logical_not(on_diagonal), core == 0)
    second_core = jnp.logical_and(jnp.logical_not(on_diagonal), core == 1)

    @pl.when(first_core)
    def _():
        s2[0:64, :] = yb[0:64, 0:LANES]
        s2[64:128, :] = yb[0:64, middle]

    @pl.when(second_core)
    def _():
        s2[0:64, :] = yb[0:64, 0:LANES]
        s2[64:96, :] = yb[64:96, middle]
        s2[96:128, :] = nothing

    @pl.when(on_diagonal)
    def _():
        s2[0:32, :] = yb[64:96, 0:LANES]
        s2[32:64, :] = yb[64:96, middle]
        s2[64:96, :] = yb[64:96, 2 * LANES :]
        s2[96:128, :] = nothing

    def r3_copy(d):
        to = lax.rem(z + d, DEPTH)
        return remote(
            s2.at[pl.ds(pl.multiple_of(to * 8, 8), 8)],
            r3.at[d - 1],
            r3s.at[d - 1],
            r3r.at[d - 1],
            z_peer(to),
        )

    send(r3_copy, DEPTH)
    receive(r3_copy, DEPTH)
    z_own = pl.ds(pl.multiple_of(z * 8, 8), 8)
    s3[z_own, :] = s2[z_own, :] + jnp.sum(r3[...], axis=0)

    def g3_copy(d):
        return remote(
            s3.at[z_own],
            s3.at[z_own],
            g3s.at[d - 1],
            g3r.at[d - 1],
            z_peer(lax.rem(z + d, DEPTH)),
        )

    send(g3_copy, DEPTH)
    receive(g3_copy, DEPTH)


    zb[...] = jnp.zeros_like(zb)

    @pl.when(first_core)
    def _():
        zb[0:64, 0:LANES] = s3[0:64, :]
        zb[0:64, middle] = s3[64:128, :]

    @pl.when(second_core)
    def _():
        zb[0:64, 0:LANES] = s3[0:64, :]
        zb[64:96, middle] = s3[64:96, :]

    @pl.when(on_diagonal)
    def _():
        zb[64:96, 0:LANES] = s3[0:32, :]
        zb[64:96, middle] = s3[32:64, :]
        zb[64:96, 2 * LANES :] = s3[64:96, :]

    z_high, z_low = split(zb[...])
    zs[0:LANES, :] = z_high
    zs[LANES:, :] = z_low
    onto = mm_t(bs[...], zs[...])
    ub[...] = (onto[:, 0:LANES] + onto[:, LANES:]).reshape(NEAR, ROWS, LANES)

    def u_copy(e):
        return remote(
            ub.at[e], urecv.at[e - 1], us.at[e - 1], ur.at[e - 1], near_peer(before(e))
        )

    send(u_copy, NEAR)

    quads = mm_t(zs[...], zs[...])
    gram = quads[0:LANES, 0:LANES] + quads[LANES:, 0:LANES]
    gram = gram + (quads[0:LANES, LANES:] + quads[LANES:, LANES:])
    row_at = lax.broadcasted_iota(jnp.int32, (RANK, LANES), 0)
    lane_at = lax.broadcasted_iota(jnp.int32, (RANK, LANES), 1)
    beside = jnp.zeros((RANK, LANES), F32)
    for k in range(3):
        here = jnp.logical_and(lane_at >= k * RANK, lane_at < (k + 1) * RANK)
        beside = jnp.where(here, gram[k * RANK : (k + 1) * RANK], beside)
    gmine[...] = beside
    gs_copy = remote(gmine, gsib, gss.at[0], gsr.at[0], sibling)
    send_one(gs_copy)
    gs_copy.wait_recv()
    g_half = pl.ds(pl.multiple_of(core * 16, 16), 16)
    gall[plane] = gmine[g_half, :] + gsib[g_half, :]

    def gp_copy(d, source):
        return remote(
            gall.at[source],
            gall.at[source],
            gps.at[d - 1],
            gpr.at[source],
            plane_peer(lax.rem(plane + d, PLANE)),
        )

    around(PLANE, lambda d: gp_copy(d, plane).start())
    pending.append(lambda: around(PLANE, lambda d: gp_copy(d, plane).wait_send()))

    receive(u_copy, NEAR)
    img_own = pl.ds(pl.multiple_of(plane * 32 + zh * 16, 16), 16)
    img[img_own, :] = ub[0] + jnp.sum(urecv[...], axis=0)
    iz_copy = remote(img.at[img_own], img.at[img_own], izs.at[0], izr.at[0], opposite)
    send_one(iz_copy)

    around(
        PLANE, lambda d: gp_copy(d, lax.rem(plane + PLANE - d, PLANE)).wait_recv()
    )
    ghalf[g_half, :] = jnp.sum(gall[...], axis=0)
    gh_copy = remote(
        ghalf.at[g_half], ghalf.at[g_half], ghs.at[0], ghr.at[0], sibling
    )
    send_one(gh_copy)
    gh_copy.wait_recv()

    left = [ghalf[...] for _ in range(3)]
    right = [(lane_at == row_at + k * RANK).astype(F32) for k in range(3)]
    for j in range(RANK - 1):
        for k in range(3):
            at = k * RANK + j
            pivot = left[k][j : j + 1, at : at + 1]
            column = left[k][:, at : at + 1] / pivot
            factor = jnp.where(row_at > j, column, 0.0)
            left[k] = left[k] - factor * left[k][j : j + 1, :]
            right[k] = right[k] - factor * right[k][j : j + 1, :]
    inverse = []
    for k in range(3):
        diagonal = jnp.sum(
            jnp.where(lane_at == row_at + k * RANK, left[k], 0.0), axis=1, keepdims=True
        )
        inverse.append(right[k] / jnp.sqrt(diagonal))
    inverse.append(jnp.zeros((RANK, LANES), F32))
    inverse = jnp.concatenate(inverse, axis=0)

    iz_copy.wait_recv()
    img_pair = pl.ds(pl.multiple_of(plane * 32, 32), 32)

    def ix_copy(d):
        return remote(
            img.at[img_pair],
            img.at[img_pair],
            ixs.at[d - 1],
            ixr.at[d - 1],
            plane_peer(lax.rem(plane + d, PLANE)),
        )

    send(ix_copy, PLANE)
    receive(ix_copy, PLANE)
    images = mm_t(img[...], inverse, HIGH) * (1.0 / GROUPS)

    img_high, img_low = split(images.T)
    for half in range(2):
        qb[half, QB_USED:QB, :] = jnp.zeros((QB - QB_USED, LANES), F32)
    for k in range(3):
        rows = slice(k * RANK, (k + 1) * RANK)
        both = jnp.concatenate([img_high[rows], img_low[rows]], axis=0)
        first = mm(both, acts[k, 0:TOK, :])
        second = mm(img_high[rows], acts[k, TOK : 2 * TOK, :])
        share = first[0:RANK] + first[RANK:] + second
        for tile in range(FFL // LANES):
            part = share[:, tile * LANES : (tile + 1) * LANES]
            for half, row, start, count in pieces(
                tile * W + k * RANK, RANK, QB_USED
            ):
                qb[half, row : row + count, :] = part[start : start + count]

    qc_copy = remote(qb.at[1 - core], qcrecv, qcs.at[0], qcr.at[0], sibling)
    send_one(qc_copy)

    pf[core, xx, yy] = s3[...]

    def g2_copy(portion, d):
        axis = 1 - portion
        at = portion * 3 + d - 1
        block = pf.at[core, xx, yy, pl.ds(portion * 64, 64)]
        to = lax.rem(side(axis) + d, SIDE)
        return remote(block, block, g2s.at[at], g2r.at[at], side_peer(axis, to))

    def line(portion, index):
        rows = pl.ds(portion * 64, 64)
        if portion == 0:
            return pf.at[core, index, pl.ds(0, SIDE), rows]
        return pf.at[core, pl.ds(0, SIDE), index, rows]

    def g1_copy(portion, d):
        at = portion * 3 + d - 1
        block = line(portion, side(portion))
        to = lax.rem(side(portion) + d, SIDE)
        return remote(block, block, g1s.at[at], g1r.at[at], side_peer(portion, to))

    def gc_copy(portion, d):
        block = line(portion, lax.rem(side(portion) + SIDE - d, SIDE))
        at = portion * SIDE + d
        return remote(block, block, gcs.at[at], gcr.at[at], sibling)

    for portion in range(2):
        for d in (2, 1, 3):
            send_one(g2_copy(portion, d))

    qc_copy.wait_recv()
    qh[...] = qb[core] + qcrecv[...]

    def zl_peer(index):
        return (index * 2 + core, mp)

    def qr_copy(d):
        to = lax.rem(zl + d, ZLO)
        return remote(
            qh.at[pl.ds(pl.multiple_of(to * QS, 8), QS)],
            qr.at[d - 1],
            qrs.at[d - 1],
            qrr.at[d - 1],
            zl_peer(to),
        )

    send(qr_copy, ZLO)

    for portion in range(2):
        for d in (1, 3, 2):
            g2_copy(portion, d).wait_recv()
        for d in (2, 1, 3):
            send_one(g1_copy(portion, d))
        send_one(gc_copy(portion, 0))

    receive(qr_copy, ZLO)
    q_own = pl.ds(pl.multiple_of(zl * QS, 8), QS)
    qf[core, q_own, :] = qh[q_own, :] + jnp.sum(qr[...], axis=0)

    def qg_copy(d):
        return remote(
            qf.at[core, q_own],
            qf.at[core, q_own],
            qgs.at[d - 1],
            qgr.at[d - 1],
            zl_peer(lax.rem(zl + d, ZLO)),
        )

    def qd_copy(d):
        rows = pl.ds(pl.multiple_of(lax.rem(zl + ZLO - d, ZLO) * QS, 8), QS)
        return remote(
            qf.at[core, rows], qf.at[core, rows], qds.at[d], qdr.at[d], sibling
        )

    send(qg_copy, ZLO)
    send_one(qd_copy(0))

    for d in (1, 3, 2):
        for portion in range(2):
            g1_copy(portion, d).wait_recv()
            send_one(gc_copy(portion, d))
    for d in range(SIDE):
        for portion in range(2):
            gc_copy(portion, d).wait_recv()

    for of_core in range(2):
        for chip in range(PLANE):
            for row, k, tile in tiles_of(of_core, chip)[1]:
                ptf[k * RANK : (k + 1) * RANK, tile * LANES : (tile + 1) * LANES] = pf[
                    of_core, chip // SIDE, chip % SIDE, row : row + RANK, :
                ]
    scaled = inverse[0:W, 0:W] * math.sqrt(D)

    def left_factor(tile, carry):
        at = pl.ds(pl.multiple_of(tile * 4 * LANES, LANES), 4 * LANES)
        pfin[:, at] = mm(scaled, ptf[:, at], HIGH)
        return carry

    lax.fori_loop(0, D // (4 * LANES), left_factor, 0)
    out_copy = pltpu.make_async_copy(pfin, p_out, outs.at[0])
    out_copy.start()
    pending.append(out_copy.wait)

    def hand_on(d):
        qg_copy(d).wait_recv()
        qd_copy(d).start()

    around(ZLO, hand_on)
    pending.append(lambda: around(ZLO, lambda d: qd_copy(d).wait_send()))
    qd_copy(0).wait_recv()
    receive(qd_copy, ZLO)

    for tile in range(FFL // LANES):
        parts = [
            qf[half, row : row + count, :]
            for half, row, _, count in pieces(tile * W, W, QB_USED)
        ]
        whole = parts[0] if len(parts) == 1 else jnp.concatenate(parts, axis=0)
        q_out[:, tile * LANES : (tile + 1) * LANES] = whole

    finish()


def on_device(inputs, out_grad, gate_pre, up_pre, hidden_grad, q_start):
    vmem = pl.BlockSpec(memory_space=pltpu.VMEM)
    far = pl.BlockSpec(memory_space=pl.ANY)
    buffers = [
        pltpu.VMEM((TOK, FFL), BF16),
        pltpu.VMEM((TOK, FFL), BF16),
        pltpu.VMEM((TOK, FFL), BF16),
        pltpu.VMEM((3, 2 * TOK, FFL), BF16),
        pltpu.VMEM((2 * LANES, FFL), BF16),
        pltpu.VMEM((TOK, LANES), F32),
        pltpu.VMEM((PLANE - 1, 32, LANES), F32),
        pltpu.VMEM((32, LANES), F32),
        pltpu.VMEM((16, LANES), F32),
        pltpu.VMEM((2 * TILES, ROWS, LANES), F32),
        pltpu.VMEM((NEAR, 3, ROWS, LANES), F32),
        pltpu.VMEM((NEAR * ROWS, 3 * LANES), BF16),
        pltpu.VMEM((NEAR, ROWS, LANES), F32),
        pltpu.VMEM((W, 3 * LANES), F32),
        pltpu.VMEM((SHARE, LANES), F32),
        pltpu.VMEM((DEPTH - 1, 8, LANES), F32),
        pltpu.VMEM((SHARE, LANES), F32),
        pltpu.VMEM((LANES, 3 * LANES), F32),
        pltpu.VMEM((2 * LANES, 3 * LANES), BF16),
        pltpu.VMEM((NEAR, ROWS, LANES), F32),
        pltpu.VMEM((NEAR - 1, ROWS, LANES), F32),
        pltpu.VMEM((RANK, LANES), F32),
        pltpu.VMEM((RANK, LANES), F32),
        pltpu.VMEM((PLANE, 16, LANES), F32),
        pltpu.VMEM((RANK, LANES), F32),
        pltpu.VMEM((2, SIDE, SIDE, SHARE, LANES), F32),
        pltpu.VMEM((W, D), F32),
        pltpu.VMEM((W, D), F32),
        pltpu.VMEM((TOK, LANES), F32),
        pltpu.VMEM((2, QB, LANES), F32),
        pltpu.VMEM((QB, LANES), F32),
        pltpu.VMEM((QB, LANES), F32),
        pltpu.VMEM((ZLO - 1, QS, LANES), F32),
        pltpu.VMEM((2, QB, LANES), F32),
    ]
    counts = [12]
    counts += [15, 15, 1, 1]
    counts += [31, 31, 31, 31]
    counts += [15, 15, 15, 15]
    counts += [31, 31]
    counts += [1, 1, 15, 16, 1, 1]
    counts += [6, 6, 6, 6, 8, 8]
    counts += [1, 1, 15, 15]
    counts += [1, 1, 7, 7, 7, 7, 8, 8]
    counts += [1]
    flags = [pltpu.SemaphoreType.DMA((count,)) for count in counts]
    p_turned, q_turned = pl.pallas_call(
        kernel,
        out_shape=(
            jax.ShapeDtypeStruct((W, D), F32),
            jax.ShapeDtypeStruct((W, FFL), F32),
        ),
        in_specs=[vmem, vmem, far, far, far, vmem],
        out_specs=(far, vmem),
        scratch_shapes=buffers + flags,
        compiler_params=pltpu.CompilerParams(
            collective_id=0, has_side_effects=True, vmem_limit_bytes=56 * 2**20
        ),
        name="power_step",
    )(inputs, out_grad, gate_pre, up_pre, hidden_grad, q_start.T)
    return p_turned.T, q_turned.T


def solution(mesh):
    in_specs = (
        P(("dp", "mp"), None),
        P(("dp", "mp"), None),
        P("dp", "mp"),
        P("dp", "mp"),
        P("dp", "mp"),
        P("mp", None),
    )
    out_specs = (P(), P("mp", None))
    return jax.shard_map(
        on_device, mesh=mesh, in_specs=in_specs, out_specs=out_specs, check_vma=False
    )
```

time: 133 us -> 115 us (0.86)
  Pallas kernels: 126 us -> 110 us
  local copies, waits for them, and re-layouts: 6.04 us -> 3.62 us
    pallas_call x1, Pallas kernels: 126 us -> 110 us  [on_device(): pl.pallas_call(kernel, out_shape=(jax.ShapeDtypeStruct((W, D), F32), jax....]
    pallas_call x2 -> x0, local copies, waits for them, and re-layouts: 3.97 us -> none  [on_device(): pl.pallas_call(kernel, out_shape=(jax.ShapeDtypeStruct((D, W), F32), jax....]
    unnamed x3 -> x4, local copies, waits for them, and re-layouts: 2.07 us -> 3.62 us
where the time goes in v2:
time: 115 us; the launch traced here: 114 us
  Pallas kernels  110 us (96%)
  local copies, waits for them, and re-layouts  3.62 us (3%)
    pallas_call x1, Pallas kernels, on_device(): pl.pallas_call(kernel, out_shape=(jax.ShapeDtypeStruct((W, D), F32), jax....  110 us
    unnamed x4, local copies, waits for them, and re-layouts  3.62 us

profile of v2, /device:TPU:1, one launch (start us, length us, event | category | flops | bytes accessed | tf_op | source)
XLA Modules:
  0.0 114.5 jit_solution(17175789951003771597)
XLA Ops:
  0.6 110.2 %power_step.1 = (f32[96,4608]{1,0:T(8,128)}, f32[96,1152]{1,0:T(8,128)}) custom-call(bf16[16,4608]{1,0:T(8,128)(2,1)} %in_ref.1, bf16[16,4608]{1,0:T(8,128)(2,1)} %og_ref.1, bf16[512,1152]{1,0:T(8,128)(2,1)} %gate_ref.1, bf16[512,1152]{1,0:T(8,128)(2,1)} %up_ref.1, bf16[512,1152]{1,0:T(8,128)(2,1)} %cot_ref.1, f32[96,1152]{1,0:T(8,128)} %bitcast.4), custom_call_target="tpu_custom_call" | custom-call | tf_op jit(solution)/shard_map/power_step/pallas_call | solution.py:783
  110.8 0.0 copy-start
  110.8 2.8 %copy.10 = f32[4608,96]{0,1:T(8,128)} copy(f32[4608,96]{0,1:T(8,128)} %bitcast.3) | data formatting | bytes 3538944
  113.7 0.0 copy-done
  113.7 0.8 copy.11
Async XLA Ops:
  110.8 2.9 %copy-start = (f32[96,1152]{1,0:T(8,128)S(1)}, f32[96,1152]{1,0:T(8,128)}, u32[]{:S(2)}) copy-start(f32[96,1152]{1,0:T(8,128)} %get-tuple-element.5) | copy-start | bytes 1327108

commit v3 on v2

v3 whole, which is shorter than its diff:
```python
import functools
import math

import jax
import jax.numpy as jnp
from jax import lax
from jax.experimental import pallas as pl
from jax.experimental.pallas import tpu as pltpu
from jax.sharding import PartitionSpec as P

MESH = pl.DeviceIdType.MESH
F32 = jnp.float32
BF16 = jnp.bfloat16
HIGH = lax.Precision.HIGHEST

D = 4608
TOK = 512
FFL = 1152
ROWS = 16
RANK = 32
W = 3 * RANK
LANES = 128
SIDE = 4
PLANE = SIDE * SIDE
ZLO = 8
DEPTH = 16
GROUPS = 16

TILES = D // LANES
NEAR = 2 * PLANE
SHARE = 128
QB = 448
QB_USED = 432
QS = QB // ZLO
HALF = TOK // 2


def split(value):
    high = value.astype(BF16)
    low = (value - high.astype(F32)).astype(BF16)
    return high, low


def mm(left, right, precision=None):
    return lax.dot_general(
        left,
        right,
        (((1,), (0,)), ((), ())),
        preferred_element_type=F32,
        precision=precision,
    )


def mm_t(left, right, precision=None):
    return lax.dot_general(
        left,
        right,
        (((1,), (1,)), ((), ())),
        preferred_element_type=F32,
        precision=precision,
    )


def tiles_of(core, plane):
    x, y = divmod(plane, SIDE)
    if x == y:
        first = 12 + 6 * x + 3 * core
        return (
            [(1, first + i) for i in range(3)],
            [(32 * i, 2, first + i) for i in range(3)],
        )
    at = plane - plane // (SIDE + 1) - 1
    if core == 0:
        return (
            [(0, 3 * at), (0, 3 * at + 1)],
            [
                (0, 0, 3 * at),
                (32, 1, 3 * at),
                (64, 0, 3 * at + 1),
                (96, 1, 3 * at + 1),
            ],
        )
    return (
        [(0, 3 * at + 2), (1, at)],
        [(0, 0, 3 * at + 2), (32, 1, 3 * at + 2), (64, 2, at)],
    )


def staged(core, plane):
    x, y = lax.div(plane, SIDE), lax.rem(plane, SIDE)
    at = plane - lax.div(plane, SIDE + 1) - 1
    return jnp.where(x == y, 48 + 6 * x + 3 * core, 4 * at + 2 * core)


def pieces(start, count, used):
    out = []
    at = start
    while at < start + count:
        block, row = divmod(at, used)
        here = min(used - row, start + count - at)
        out.append((block, row, at - start, here))
        at += here
    return out


def kernel(
    in_ref,
    og_ref,
    gate_ref,
    up_ref,
    cot_ref,
    q_ref,
    p_out,
    q_out,
    gate_in,
    up_in,
    cot_in,
    acts,
    qs,
    mpart,
    mrecv,
    maway,
    mzrecv,
    bst,
    bt,
    bs,
    mall,
    yb,
    s2,
    r3,
    s3,
    zb,
    zs,
    ub,
    urecv,
    gmine,
    gsib,
    gall,
    ghalf,
    pf,
    ptf,
    pfin,
    img,
    qb,
    qcrecv,
    qh,
    qr,
    qf,
    loads,
    ms,
    mr,
    mzs,
    mzr,
    bsend,
    brecv,
    mas,
    mar,
    r3s,
    r3r,
    g3s,
    g3r,
    us,
    ur,
    gss,
    gsr,
    gps,
    gpr,
    ghs,
    ghr,
    g2s,
    g2r,
    g1s,
    g1r,
    gcs,
    gcr,
    izs,
    izr,
    ixs,
    ixr,
    qcs,
    qcr,
    qrs,
    qrr,
    qgs,
    qgr,
    qds,
    qdr,
    outs,
):
    dp, mp = lax.axis_index("dp"), lax.axis_index("mp")
    core, zl = lax.rem(dp, 2), lax.div(dp, 2)
    zh, plane = lax.rem(mp, 2), lax.div(mp, 2)
    xx, yy = lax.div(plane, SIDE), lax.rem(plane, SIDE)
    z = zh * ZLO + zl
    on_diagonal = xx == yy
    sibling = (zl * 2 + 1 - core, mp)
    opposite = (dp, plane * 2 + 1 - zh)

    def plane_peer(index):
        return (dp, index * 2 + zh)

    def z_peer(index):
        return (lax.rem(index, ZLO) * 2 + core, plane * 2 + lax.div(index, ZLO))

    def side_peer(axis, index):
        along_x = (dp, (index * SIDE + yy) * 2 + zh)
        along_y = (dp, (xx * SIDE + index) * 2 + zh)
        return along_x if axis == 0 else along_y

    def side(axis):
        return xx if axis == 0 else yy

    def after(e):
        x = lax.rem(xx + lax.div(lax.rem(e, PLANE), SIDE), SIDE)
        y = lax.rem(yy + lax.rem(e, SIDE), SIDE)
        return lax.rem(core + lax.div(e, PLANE), 2), x * SIDE + y

    def before(e):
        x = lax.rem(xx + SIDE - lax.div(lax.rem(e, PLANE), SIDE), SIDE)
        y = lax.rem(yy + SIDE - lax.rem(e, SIDE), SIDE)
        return lax.rem(core + lax.div(e, PLANE), 2), x * SIDE + y

    def near_peer(place):
        return (zl * 2 + place[0], place[1] * 2 + zh)

    def remote(src, dst, send, recv, to):
        return pltpu.make_async_remote_copy(
            src_ref=src,
            dst_ref=dst,
            send_sem=send,
            recv_sem=recv,
            device_id=to,
            device_id_type=MESH,
        )

    def around(count, body, first=1):
        def step(index, carry):
            body(index)
            return carry

        lax.fori_loop(first, count, step, 0)

    pending = []

    def far_first(count, body):
        if count == NEAR:

            def step(i):
                d = 1 + lax.rem(25 - i, 15)
                body(d)
                body(PLANE + d)

            around(15, step, first=0)
            body(jnp.int32(PLANE))
        elif count == PLANE:
            around(15, lambda i: body(1 + lax.rem(25 - i, 15)), first=0)
        else:
            half = count // 2
            around(
                count - 1,
                lambda i: body(
                    half + (1 - 2 * lax.rem(i, 2)) * lax.div(i + 1, 2)
                ),
                first=0,
            )

    def drain(bytes_of, semaphore):
        pltpu.make_async_copy(bytes_of, bytes_of, semaphore).wait()

    def send(make, count, bytes_of, semaphore):
        far_first(count, lambda d: make(d).start())
        pending.append(lambda: drain(bytes_of, semaphore))

    def send_one(copy):
        copy.start()
        pending.append(copy.wait_send)

    def finish():
        while pending:
            pending.pop(0)()

    barrier = pltpu.get_barrier_semaphore()

    def greet(to):
        pl.semaphore_signal(barrier, inc=1, device_id=to, device_id_type=MESH)

    around(DEPTH, lambda d: greet(z_peer(lax.rem(z + d, DEPTH))))
    around(NEAR, lambda e: greet(near_peer(after(e))))

    quarter = PLANE // 2

    def load(half, part, which):
        chips = pl.ds(part * quarter, quarter)
        src, dst = (
            (gate_ref, gate_in),
            (up_ref, up_in),
            (cot_ref, cot_in),
        )[which]
        return pltpu.make_async_copy(
            src.at[chips, zh if half else 1 - zh],
            dst.at[half, chips],
            loads.at[half * 6 + part * 3 + which],
        )

    for half in range(2):
        for part in range(2):
            for which in range(3):
                load(half, part, which).start()

    place = 0
    for chip_type in (False, True):
        for chip in range(PLANE):
            if (chip // SIDE == chip % SIDE) != chip_type:
                continue
            for of_core in range(2):
                for array, tile in tiles_of(of_core, chip)[0]:
                    source = (in_ref, og_ref)[array]
                    bst[place] = source[:, tile * LANES : (tile + 1) * LANES].astype(F32)
                    place += 1

    def activate(half, i):
        rows = pl.ds(pl.multiple_of(i * ROWS, ROWS), ROWS)
        g = gate_in[half, i].astype(F32)
        u = up_in[half, i].astype(F32)
        e = cot_in[half, i].astype(F32)
        s = 1.0 / (1.0 + jnp.exp(-g))
        silu = g * s
        values = (e * u * s * (1.0 + g * (1.0 - s)), e * silu, silu * u)
        for k, value in enumerate(values):
            high, low = split(value)
            acts[k, half, 0, rows, :] = high
            acts[k, half, 1, rows, :] = low

    def b_copy(e, count):
        to = after(e)
        return remote(
            bst.at[pl.ds(staged(*to), count)],
            bt.at[e, pl.ds(0, count)],
            bsend.at[0],
            brecv.at[lax.div(e, PLANE)],
            near_peer(to),
        )

    def b_each(e, act, diagonal):
        @pl.when(diagonal)
        def _():
            act(b_copy(e, 3))

        @pl.when(jnp.logical_not(diagonal))
        def _():
            act(b_copy(e, 2))

    def to_diagonal(e):
        chip = after(e)[1]
        return lax.div(chip, SIDE) == lax.rem(chip, SIDE)

    q_high, q_low = split(q_ref[...])
    qs[...] = jnp.zeros_like(qs)
    qs[0:W, :] = q_high
    qs[LANES : LANES + W, :] = q_low

    lane = lax.broadcasted_iota(jnp.int32, (HALF, LANES), 1)

    def mix(half):
        for k in range(3):
            first = mm_t(acts[k, half, 0], qs[...])
            second = mm_t(acts[k, half, 1], qs[0:LANES, :])
            both = first[:, 0:LANES] + first[:, LANES:] + second
            if k == 0:
                mpart[half] = both
            else:
                mpart[half] = jnp.where(lane >= k * RANK, both, mpart[half])

    plane_rows = pl.ds(pl.multiple_of(plane * ROWS, ROWS), ROWS)

    def m_copy(half, d):
        to = after(d)[1]
        return remote(
            mpart.at[half, pl.ds(pl.multiple_of(to * ROWS, ROWS), ROWS)],
            mrecv.at[half, d - 1],
            ms.at[half],
            mr.at[half],
            plane_peer(to),
        )

    def m_send(half):
        send(lambda d: m_copy(half, d), PLANE, mrecv.at[half], ms.at[half])

    def m_sum(half):
        drain(mrecv.at[half], mr.at[half])
        return mpart[half, plane_rows, :] + jnp.sum(mrecv[half], axis=0)

    for half in range(2):
        for part in range(2):
            for which in range(3):
                load(half, part, which).wait()
            around(
                (part + 1) * quarter,
                lambda i: activate(half, i),
                first=part * quarter,
            )
        mix(half)
        if half == 0:
            pl.semaphore_wait(barrier, DEPTH - 1 + NEAR - 1)
        m_send(half)
        if half == 0:
            around(PLANE, lambda e: b_each(e, lambda c: c.start(), to_diagonal(e)))
    maway[...] = m_sum(0)
    mz_copy = remote(maway, mzrecv, mzs.at[0], mzr.at[0], opposite)
    send_one(mz_copy)
    around(
        NEAR, lambda e: b_each(e, lambda c: c.start(), to_diagonal(e)), first=PLANE
    )

    def b_sent():
        for count, here in ((3, on_diagonal), (2, jnp.logical_not(on_diagonal))):

            @pl.when(here)
            def _():
                drain(bst.at[pl.ds(0, 2 * TILES - count)], bsend.at[0])

    pending.append(b_sent)

    def b_receive(group):
        slots = pl.ds(1, PLANE - 1) if group == 0 else pl.ds(PLANE, PLANE)
        for count, here in ((3, on_diagonal), (2, jnp.logical_not(on_diagonal))):

            @pl.when(here)
            def _():
                drain(bt.at[slots, pl.ds(0, count)], brecv.at[group])

    mhome = m_sum(1)

    own_tiles = staged(core, plane)
    for tile in range(2):
        bt[0, tile] = bst[own_tiles + tile]

    @pl.when(on_diagonal)
    def _():
        bt[0, 2] = bst[own_tiles + 2]

    def round_rows(e):
        rows = pl.ds(pl.multiple_of(e * ROWS, ROWS), ROWS)
        for tile in range(2):
            bs[rows, tile * LANES : (tile + 1) * LANES] = bt[e, tile].astype(BF16)

        @pl.when(on_diagonal)
        def _():
            bs[rows, 2 * LANES :] = bt[e, 2].astype(BF16)

        @pl.when(jnp.logical_not(on_diagonal))
        def _():
            bs[rows, 2 * LANES :] = jnp.zeros((ROWS, LANES), BF16)

    b_receive(0)
    around(PLANE, round_rows, first=0)

    mz_copy.wait_recv()
    mall[0] = (mhome + mzrecv[...]) * (1.0 / GROUPS)

    def ma_copy(e):
        return remote(
            mall.at[0], mall.at[e], mas.at[0], mar.at[0], near_peer(after(e))
        )

    ma_bytes = mall.at[pl.ds(1, NEAR - 1)]
    send(ma_copy, NEAR, ma_bytes, mas.at[0])

    b_receive(1)
    around(NEAR, round_rows, first=PLANE)
    drain(ma_bytes, mar.at[0])

    m_turned = mall[...].reshape(NEAR * ROWS, LANES).T
    m_high, m_low = split(m_turned[0:W])
    both = mm(jnp.concatenate([m_high, m_low], axis=0), bs[...])
    yb[...] = both[0:W] + both[W:]
    middle = slice(LANES, 2 * LANES)
    nothing = jnp.zeros((RANK, LANES), F32)
    first_core = jnp.logical_and(jnp.logical_not(on_diagonal), core == 0)
    second_core = jnp.logical_and(jnp.logical_not(on_diagonal), core == 1)

    @pl.when(first_core)
    def _():
        s2[0:64, :] = yb[0:64, 0:LANES]
        s2[64:128, :] = yb[0:64, middle]

    @pl.when(second_core)
    def _():
        s2[0:64, :] = yb[0:64, 0:LANES]
        s2[64:96, :] = yb[64:96, middle]
        s2[96:128, :] = nothing

    @pl.when(on_diagonal)
    def _():
        s2[0:32, :] = yb[64:96, 0:LANES]
        s2[32:64, :] = yb[64:96, middle]
        s2[64:96, :] = yb[64:96, 2 * LANES :]
        s2[96:128, :] = nothing

    def r3_copy(d):
        to = lax.rem(z + d, DEPTH)
        return remote(
            s2.at[pl.ds(pl.multiple_of(to * 8, 8), 8)],
            r3.at[d - 1],
            r3s.at[0],
            r3r.at[0],
            z_peer(to),
        )

    send(r3_copy, DEPTH, r3, r3s.at[0])
    drain(r3, r3r.at[0])
    z_own = pl.ds(pl.multiple_of(z * 8, 8), 8)
    s3[z_own, :] = s2[z_own, :] + jnp.sum(r3[...], axis=0)

    def g3_copy(d):
        return remote(
            s3.at[z_own],
            s3.at[z_own],
            g3s.at[0],
            g3r.at[0],
            z_peer(lax.rem(z + d, DEPTH)),
        )

    g3_bytes = s3.at[pl.ds(0, SHARE - 8)]
    send(g3_copy, DEPTH, g3_bytes, g3s.at[0])
    drain(g3_bytes, g3r.at[0])


    zb[...] = jnp.zeros_like(zb)

    @pl.when(first_core)
    def _():
        zb[0:64, 0:LANES] = s3[0:64, :]
        zb[0:64, middle] = s3[64:128, :]

    @pl.when(second_core)
    def _():
        zb[0:64, 0:LANES] = s3[0:64, :]
        zb[64:96, middle] = s3[64:96, :]

    @pl.when(on_diagonal)
    def _():
        zb[64:96, 0:LANES] = s3[0:32, :]
        zb[64:96, middle] = s3[32:64, :]
        zb[64:96, 2 * LANES :] = s3[64:96, :]

    z_high, z_low = split(zb[...])
    zs[0:LANES, :] = z_high
    zs[LANES:, :] = z_low
    onto = mm_t(bs[...], zs[...])
    ub[...] = (onto[:, 0:LANES] + onto[:, LANES:]).reshape(NEAR, ROWS, LANES)

    def u_copy(e):
        return remote(
            ub.at[e], urecv.at[e - 1], us.at[0], ur.at[0], near_peer(before(e))
        )

    send(u_copy, NEAR, urecv, us.at[0])

    pf[core, xx, yy] = s3[...]

    def g2_copy(portion, d):
        axis = 1 - portion
        at = portion * 3 + d - 1
        block = pf.at[core, xx, yy, pl.ds(portion * 64, 64)]
        to = lax.rem(side(axis) + d, SIDE)
        return remote(block, block, g2s.at[at], g2r.at[at], side_peer(axis, to))

    def line(portion, index):
        rows = pl.ds(portion * 64, 64)
        if portion == 0:
            return pf.at[core, index, pl.ds(0, SIDE), rows]
        return pf.at[core, pl.ds(0, SIDE), index, rows]

    def g1_copy(portion, d):
        at = portion * 3 + d - 1
        block = line(portion, side(portion))
        to = lax.rem(side(portion) + d, SIDE)
        return remote(block, block, g1s.at[at], g1r.at[at], side_peer(portion, to))

    for portion in range(2):
        for d in (2, 1, 3):
            send_one(g2_copy(portion, d))


    quads = mm_t(zs[...], zs[...])
    gram = quads[0:LANES, 0:LANES] + quads[LANES:, 0:LANES]
    gram = gram + (quads[0:LANES, LANES:] + quads[LANES:, LANES:])
    row_at = lax.broadcasted_iota(jnp.int32, (RANK, LANES), 0)
    lane_at = lax.broadcasted_iota(jnp.int32, (RANK, LANES), 1)
    beside = jnp.zeros((RANK, LANES), F32)
    for k in range(3):
        here = jnp.logical_and(lane_at >= k * RANK, lane_at < (k + 1) * RANK)
        beside = jnp.where(here, gram[k * RANK : (k + 1) * RANK], beside)
    gmine[...] = beside
    gs_copy = remote(gmine, gsib, gss.at[0], gsr.at[0], sibling)
    send_one(gs_copy)
    gs_copy.wait_recv()
    g_half = pl.ds(pl.multiple_of(core * 16, 16), 16)
    gall[plane] = gmine[g_half, :] + gsib[g_half, :]

    def gp_copy(d):
        return remote(
            gall.at[plane],
            gall.at[plane],
            gps.at[0],
            gpr.at[0],
            plane_peer(after(d)[1]),
        )

    far_first(PLANE, lambda d: gp_copy(d).start())
    gp_bytes = gall.at[pl.ds(0, PLANE - 1)]
    pending.append(lambda: drain(gp_bytes, gps.at[0]))

    drain(urecv, ur.at[0])
    img[1, plane_rows, :] = ub[0] + jnp.sum(urecv[...], axis=0)
    iz_copy = remote(
        img.at[1, plane_rows], img.at[0, plane_rows], izs.at[0], izr.at[0], opposite
    )
    send_one(iz_copy)

    def ix_copy(half, d):
        return remote(
            img.at[half, plane_rows],
            img.at[half, plane_rows],
            ixs.at[half],
            ixr.at[half],
            plane_peer(after(d)[1]),
        )

    def ix_bytes(half):
        return img.at[half, pl.ds(0, HALF - ROWS)]

    def ix_send(half):
        send(lambda d: ix_copy(half, d), PLANE, ix_bytes(half), ixs.at[half])

    def ix_receive(half):
        drain(ix_bytes(half), ixr.at[half])

    ix_send(1)

    for portion in range(2):
        for d in (1, 3, 2):
            g2_copy(portion, d).wait_recv()
        for d in (2, 1, 3):
            send_one(g1_copy(portion, d))

    drain(gp_bytes, gpr.at[0])
    ghalf[g_half, :] = jnp.sum(gall[...], axis=0)
    gh_copy = remote(
        ghalf.at[g_half], ghalf.at[g_half], ghs.at[0], ghr.at[0], sibling
    )
    send_one(gh_copy)
    gh_copy.wait_recv()

    left = [ghalf[...] for _ in range(3)]
    right = [(lane_at == row_at + k * RANK).astype(F32) for k in range(3)]
    def eliminate(j):
        for k in range(3):
            at = k * RANK + j
            pivot = left[k][j : j + 1, at : at + 1]
            column = left[k][:, at : at + 1] / pivot
            factor = jnp.where(row_at > j, column, 0.0)
            left[k] = left[k] - factor * left[k][j : j + 1, :]
            right[k] = right[k] - factor * right[k][j : j + 1, :]

    middle_step = RANK // 2
    for j in range(middle_step):
        eliminate(j)
    iz_copy.wait_recv()
    ix_send(0)
    for j in range(middle_step, RANK - 1):
        eliminate(j)
    inverse = []
    for k in range(3):
        diagonal = jnp.sum(
            jnp.where(lane_at == row_at + k * RANK, left[k], 0.0), axis=1, keepdims=True
        )
        inverse.append(right[k] / jnp.sqrt(diagonal))
    inverse.append(jnp.zeros((RANK, LANES), F32))
    inverse = jnp.concatenate(inverse, axis=0)

    for side_half in range(2):
        qb[side_half, QB_USED:QB, :] = jnp.zeros((QB - QB_USED, LANES), F32)
    for half in (1, 0):
        ix_receive(half)
        if half == 0:
            for portion in range(2):
                for d in (1, 3, 2):
                    g1_copy(portion, d).wait_recv()
            gc_copy = remote(
                pf.at[core], pf.at[core], gcs.at[0], gcr.at[0], sibling
            )
            send_one(gc_copy)
        images = mm_t(img[half], inverse, HIGH) * (1.0 / GROUPS)
        img_high, img_low = split(images.T)
        for k in range(3):
            rows = slice(k * RANK, (k + 1) * RANK)
            both = jnp.concatenate([img_high[rows], img_low[rows]], axis=0)
            first = mm(both, acts[k, half, 0])
            second = mm(img_high[rows], acts[k, half, 1])
            share = first[0:RANK] + first[RANK:] + second
            for tile in range(FFL // LANES):
                part = share[:, tile * LANES : (tile + 1) * LANES]
                for block, row, start, count in pieces(
                    tile * W + k * RANK, RANK, QB_USED
                ):
                    piece = part[start : start + count]
                    if half == 0:
                        piece = piece + qb[block, row : row + count, :]
                    qb[block, row : row + count, :] = piece

    qc_copy = remote(qb.at[1 - core], qcrecv, qcs.at[0], qcr.at[0], sibling)
    send_one(qc_copy)

    qc_copy.wait_recv()
    qh[...] = qb[core] + qcrecv[...]

    def zl_peer(index):
        return (index * 2 + core, mp)

    def q_rows(index):
        return pl.ds(pl.multiple_of(index * QS, 8), QS)

    def qr_copy(d):
        to = lax.rem(zl + d, ZLO)
        return remote(
            qh.at[q_rows(to)], qr.at[d - 1], qrs.at[0], qrr.at[0], zl_peer(to)
        )

    send(qr_copy, ZLO, qr, qrs.at[0])

    gc_copy.wait_recv()

    for of_core in range(2):
        for chip in range(PLANE):
            for row, k, tile in tiles_of(of_core, chip)[1]:
                ptf[k * RANK : (k + 1) * RANK, tile * LANES : (tile + 1) * LANES] = pf[
                    of_core, chip // SIDE, chip % SIDE, row : row + RANK, :
                ]
    scaled = inverse[0:W, 0:W] * math.sqrt(D)

    def left_factor(tile, carry):
        at = pl.ds(pl.multiple_of(tile * 4 * LANES, LANES), 4 * LANES)
        pfin[:, at] = mm(scaled, ptf[:, at], HIGH)
        return carry

    lax.fori_loop(0, D // (4 * LANES), left_factor, 0)
    out_copy = pltpu.make_async_copy(pfin, p_out, outs.at[0])
    out_copy.start()
    pending.append(out_copy.wait)

    finish()

    drain(qr, qrr.at[0])
    q_own = q_rows(zl)
    qf[core, q_own, :] = qh[q_own, :] + jnp.sum(qr[...], axis=0)

    def qg_copy(d):
        own = qf.at[core, q_own]
        to = zl_peer(lax.rem(zl + d, ZLO))
        return remote(own, own, qgs.at[0], qgr.at[0], to)

    qg_bytes = qf.at[core, pl.ds(0, QB - QS)]
    send(qg_copy, ZLO, qg_bytes, qgs.at[0])
    drain(qg_bytes, qgr.at[0])
    qd_copy = remote(qf.at[core], qf.at[core], qds.at[0], qdr.at[0], sibling)
    send_one(qd_copy)
    qd_copy.wait_recv()

    for tile in range(FFL // LANES):
        parts = [
            qf[half, row : row + count, :]
            for half, row, _, count in pieces(tile * W, W, QB_USED)
        ]
        whole = parts[0] if len(parts) == 1 else jnp.concatenate(parts, axis=0)
        q_out[:, tile * LANES : (tile + 1) * LANES] = whole

    finish()


def deliver(p_ref, q_ref, p_out, q_out, p_held, q_held, come, go):
    count = 6
    rows = [pl.ds(i * (W // count), W // count) for i in range(count)]
    arrays = [(p_ref, p_held, p_out, part) for part in rows]
    arrays.append((q_ref, q_held, q_out, pl.ds(0, W)))
    into = [
        pltpu.make_async_copy(src.at[part], held.at[part], come.at[i])
        for i, (src, held, _, part) in enumerate(arrays)
    ]
    out = [
        pltpu.make_async_copy(held.at[part], dst.at[part], go.at[i])
        for i, (_, held, dst, part) in enumerate(arrays)
    ]
    for copy in into:
        copy.start()
    for first, second in zip(into, out):
        first.wait()
        second.start()
    for copy in out:
        copy.wait()


def on_device(inputs, out_grad, gate_pre, up_pre, hidden_grad, q_start):
    vmem = pl.BlockSpec(memory_space=pltpu.VMEM)
    far = pl.BlockSpec(memory_space=pl.ANY)
    buffers = [
        pltpu.VMEM((2, PLANE, ROWS, FFL), BF16),
        pltpu.VMEM((2, PLANE, ROWS, FFL), BF16),
        pltpu.VMEM((2, PLANE, ROWS, FFL), BF16),
        pltpu.VMEM((3, 2, 2, HALF, FFL), BF16),
        pltpu.VMEM((2 * LANES, FFL), BF16),
        pltpu.VMEM((2, HALF, LANES), F32),
        pltpu.VMEM((2, PLANE - 1, ROWS, LANES), F32),
        pltpu.VMEM((ROWS, LANES), F32),
        pltpu.VMEM((16, LANES), F32),
        pltpu.VMEM((2 * TILES, ROWS, LANES), F32),
        pltpu.VMEM((NEAR, 3, ROWS, LANES), F32),
        pltpu.VMEM((NEAR * ROWS, 3 * LANES), BF16),
        pltpu.VMEM((NEAR, ROWS, LANES), F32),
        pltpu.VMEM((W, 3 * LANES), F32),
        pltpu.VMEM((SHARE, LANES), F32),
        pltpu.VMEM((DEPTH - 1, 8, LANES), F32),
        pltpu.VMEM((SHARE, LANES), F32),
        pltpu.VMEM((LANES, 3 * LANES), F32),
        pltpu.VMEM((2 * LANES, 3 * LANES), BF16),
        pltpu.VMEM((NEAR, ROWS, LANES), F32),
        pltpu.VMEM((NEAR - 1, ROWS, LANES), F32),
        pltpu.VMEM((RANK, LANES), F32),
        pltpu.VMEM((RANK, LANES), F32),
        pltpu.VMEM((PLANE, 16, LANES), F32),
        pltpu.VMEM((RANK, LANES), F32),
        pltpu.VMEM((2, SIDE, SIDE, SHARE, LANES), F32),
        pltpu.VMEM((W, D), F32),
        pltpu.VMEM((W, D), F32),
        pltpu.VMEM((2, HALF, LANES), F32),
        pltpu.VMEM((2, QB, LANES), F32),
        pltpu.VMEM((QB, LANES), F32),
        pltpu.VMEM((QB, LANES), F32),
        pltpu.VMEM((ZLO - 1, QS, LANES), F32),
        pltpu.VMEM((2, QB, LANES), F32),
    ]
    counts = [12]
    counts += [2, 2, 1, 1]
    counts += [1, 2, 1, 1]
    counts += [1, 1, 1, 1]
    counts += [1, 1]
    counts += [1, 1, 1, 1, 1, 1]
    counts += [6, 6, 6, 6, 1, 1]
    counts += [1, 1, 2, 2]
    counts += [1, 1, 1, 1, 1, 1, 1, 1]
    counts += [1]
    flags = [pltpu.SemaphoreType.DMA((count,)) for count in counts]
    by_half = [
        array.reshape(PLANE, 2, ROWS, FFL) for array in (gate_pre, up_pre, hidden_grad)
    ]
    p_turned, q_turned = pl.pallas_call(
        kernel,
        out_shape=(
            jax.ShapeDtypeStruct((W, D), F32),
            jax.ShapeDtypeStruct((W, FFL), F32),
        ),
        in_specs=[vmem, vmem, far, far, far, vmem],
        out_specs=(far, vmem),
        scratch_shapes=buffers + flags,
        compiler_params=pltpu.CompilerParams(
            collective_id=0, has_side_effects=True, vmem_limit_bytes=56 * 2**20
        ),
        name="power_step",
    )(inputs, out_grad, *by_half, q_start.T)
    shapes = (
        jax.ShapeDtypeStruct((W, D), F32),
        jax.ShapeDtypeStruct((W, FFL), F32),
    )
    p_turned, q_turned = pl.pallas_call(
        deliver,
        out_shape=shapes,
        in_specs=[far, far],
        out_specs=(far, far),
        scratch_shapes=[
            pltpu.VMEM((W, D), F32),
            pltpu.VMEM((W, FFL), F32),
            pltpu.SemaphoreType.DMA((7,)),
            pltpu.SemaphoreType.DMA((7,)),
        ],
        compiler_params=pltpu.CompilerParams(vmem_limit_bytes=56 * 2**20),
        name="deliver",
    )(p_turned, q_turned)
    return p_turned.T, q_turned.T


def solution(mesh):
    in_specs = (
        P(("dp", "mp"), None),
        P(("dp", "mp"), None),
        P("dp", "mp"),
        P("dp", "mp"),
        P("dp", "mp"),
        P("mp", None),
    )
    out_specs = (P(), P("mp", None))
    return jax.shard_map(
        on_device, mesh=mesh, in_specs=in_specs, out_specs=out_specs, check_vma=False
    )
```

time: 115 us -> 102 us (0.89)
  Pallas kernels: 110 us -> 102 us
  local copies, waits for them, and re-layouts: 3.62 us -> 0 us
    pallas_call x1, Pallas kernels: 110 us -> 99.2 us  [on_device(): pl.pallas_call(kernel, out_shape=(jax.ShapeDtypeStruct((W, D), F32), jax....]
    unnamed x4 -> x0, local copies, waits for them, and re-layouts: 3.62 us -> none
    pallas_call x0 -> x1, Pallas kernels: none -> 2.43 us  [on_device(): pl.pallas_call(deliver, out_shape=shapes, in_specs=[far, far], out_specs=...]
where the time goes in v3:
time: 102 us
  Pallas kernels  102 us (100%)
    pallas_call x1, Pallas kernels, on_device(): pl.pallas_call(kernel, out_shape=(jax.ShapeDtypeStruct((W, D), F32), jax....  99.2 us
    pallas_call x1, Pallas kernels, on_device(): pl.pallas_call(deliver, out_shape=shapes, in_specs=[far, far], out_specs=...  2.43 us

profile of v3, /device:TPU:1, one launch (start us, length us, event | category | flops | bytes accessed | tf_op | source)
XLA Modules:
  0.0 102.3 jit_solution(14426278803048374343)
XLA Ops:
  0.6 99.2 %power_step.1 = (f32[96,4608]{1,0:T(8,128)}, f32[96,1152]{1,0:T(8,128)}) custom-call(bf16[16,4608]{1,0:T(8,128)(2,1)} %in_ref.1, bf16[16,4608]{1,0:T(8,128)(2,1)} %og_ref.1, bf16[16,2,16,1152]{3,2,1,0:T(8,128)(2,1)} %bitcast.6, bf16[16,2,16,1152]{3,2,1,0:T(8,128)(2,1)} %bitcast.7, bf16[16,2,16,1152]{3,2,1,0:T(8,128)(2,1)} %bitcast.8, f32[96,1152]{1,0:T(8,128)} %bitcast.9), custom_call_target="tpu_custom_call" | custom-call | tf_op jit(solution)/shard_map/power_step/pallas_call | solution.py:857
  99.8 2.4 %deliver.1 = (f32[96,4608]{1,0:T(8,128)}, f32[96,1152]{1,0:T(8,128)}) custom-call(f32[96,4608]{1,0:T(8,128)} %get-tuple-element.6.p_ref, f32[96,1152]{1,0:T(8,128)} %get-tuple-element.7.q_ref), custom_call_target="tpu_custom_call" | custom-call | tf_op jit(solution)/shard_map/deliver/pallas_call | solution.py:875

commit v4 on v3

--- a/solution.py
+++ b/solution.py
@@ -139,12 +139,13 @@
     ghalf,
     pf,
     ptf,
-    pfin,
     img,
     qb,
     qcrecv,
     qh,
     qr,
+    qx,
+    qy,
     qf,
     loads,
     ms,
@@ -185,7 +186,6 @@
     qgr,
     qds,
     qdr,
-    outs,
 ):
     dp, mp = lax.axis_index("dp"), lax.axis_index("mp")
     core, zl = lax.rem(dp, 2), lax.div(dp, 2)
@@ -250,8 +250,9 @@
                 body(d)
                 body(PLANE + d)
 
-            around(15, step, first=0)
             body(jnp.int32(PLANE))
+            around(15, lambda i: body(PLANE + 1 + lax.rem(25 - i, 15)), first=0)
+            around(15, lambda i: body(1 + lax.rem(25 - i, 15)), first=0)
         elif count == PLANE:
             around(15, lambda i: body(1 + lax.rem(25 - i, 15)), first=0)
         else:
@@ -722,13 +723,32 @@
     def q_rows(index):
         return pl.ds(pl.multiple_of(index * QS, 8), QS)
 
-    def qr_copy(d):
-        to = lax.rem(zl + d, ZLO)
+    across = lax.rem(zl + 4, ZLO)
+    run_start = zl - lax.rem(zl, 4)
+
+    def in_run(d):
+        return run_start + lax.rem(zl + d, 4)
+
+    def qr_copy(d, far):
+        to = in_run(d)
+        owner = lax.rem(to + 4, ZLO) if far else to
         return remote(
-            qh.at[q_rows(to)], qr.at[d - 1], qrs.at[0], qrr.at[0], zl_peer(to)
-        )
-
-    send(qr_copy, ZLO, qr, qrs.at[0])
+            qh.at[q_rows(owner)],
+            qr.at[far, d - 1],
+            qrs.at[far],
+            qrr.at[far],
+            zl_peer(to),
+        )
+
+    for far_chunk in (1, 0):
+        for d in (2, 3, 1):
+            qr_copy(d, far_chunk).start()
+
+    q_own, q_across = q_rows(zl), q_rows(across)
+    drain(qr.at[1], qrr.at[1])
+    qx[...] = qh[q_across, :] + jnp.sum(qr[1], axis=0)
+    qx_copy = remote(qx, qy, qrs.at[2], qrr.at[2], zl_peer(across))
+    send_one(qx_copy)
 
     gc_copy.wait_recv()
 
@@ -742,31 +762,46 @@
 
     def left_factor(tile, carry):
         at = pl.ds(pl.multiple_of(tile * 4 * LANES, LANES), 4 * LANES)
-        pfin[:, at] = mm(scaled, ptf[:, at], HIGH)
+        p_out[:, at] = mm(scaled, ptf[:, at], HIGH)
         return carry
 
     lax.fori_loop(0, D // (4 * LANES), left_factor, 0)
-    out_copy = pltpu.make_async_copy(pfin, p_out, outs.at[0])
-    out_copy.start()
-    pending.append(out_copy.wait)
 
     finish()
 
-    drain(qr, qrr.at[0])
-    q_own = q_rows(zl)
-    qf[core, q_own, :] = qh[q_own, :] + jnp.sum(qr[...], axis=0)
-
-    def qg_copy(d):
-        own = qf.at[core, q_own]
-        to = zl_peer(lax.rem(zl + d, ZLO))
-        return remote(own, own, qgs.at[0], qgr.at[0], to)
-
-    qg_bytes = qf.at[core, pl.ds(0, QB - QS)]
-    send(qg_copy, ZLO, qg_bytes, qgs.at[0])
-    drain(qg_bytes, qgr.at[0])
-    qd_copy = remote(qf.at[core], qf.at[core], qds.at[0], qdr.at[0], sibling)
-    send_one(qd_copy)
-    qd_copy.wait_recv()
+    drain(qr.at[0], qrr.at[0])
+    for far_chunk in range(2):
+        drain(qr.at[far_chunk], qrs.at[far_chunk])
+    qx_copy.wait_recv()
+    qf[core, q_own, :] = qh[q_own, :] + jnp.sum(qr[0], axis=0) + qy[...]
+
+    def qg_copy(rows, kind, to):
+        block = qf.at[core, rows]
+        return remote(block, block, qgs.at[kind], qgr.at[kind], zl_peer(to))
+
+    def run_rows(start):
+        return qf.at[core, pl.ds(pl.multiple_of(start * QS, 8), 4 * QS)]
+
+    def qd_copy(start, kind):
+        block = run_rows(start)
+        return remote(block, block, qds.at[kind], qdr.at[kind], sibling)
+
+    qa_copy = qg_copy(q_own, 2, across)
+    send_one(qa_copy)
+    for d in (2, 3, 1):
+        qg_copy(q_own, 0, in_run(d)).start()
+    qa_copy.wait_recv()
+    for d in (2, 3, 1):
+        qg_copy(q_across, 1, in_run(d)).start()
+    run_bytes = qr.at[0]
+    drain(run_bytes, qgr.at[0])
+    send_one(qd_copy(run_start, 0))
+    drain(run_bytes, qgr.at[1])
+    send_one(qd_copy(4 - run_start, 1))
+    for kind in range(2):
+        drain(run_bytes, qgs.at[kind])
+    for kind in range(2):
+        qd_copy(run_start, kind).wait_recv()
 
     for tile in range(FFL // LANES):
         parts = [
@@ -779,25 +814,17 @@
     finish()
 
 
-def deliver(p_ref, q_ref, p_out, q_out, p_held, q_held, come, go):
+def deliver(p_ref, q_ref, p_out, q_out, go):
     count = 6
-    rows = [pl.ds(i * (W // count), W // count) for i in range(count)]
-    arrays = [(p_ref, p_held, p_out, part) for part in rows]
-    arrays.append((q_ref, q_held, q_out, pl.ds(0, W)))
-    into = [
-        pltpu.make_async_copy(src.at[part], held.at[part], come.at[i])
-        for i, (src, held, _, part) in enumerate(arrays)
+    parts = [pl.ds(i * (W // count), W // count) for i in range(count)]
+    copies = [
+        pltpu.make_async_copy(p_ref.at[part], p_out.at[part], go.at[i])
+        for i, part in enumerate(parts)
     ]
-    out = [
-        pltpu.make_async_copy(held.at[part], dst.at[part], go.at[i])
-        for i, (_, held, dst, part) in enumerate(arrays)
-    ]
-    for copy in into:
+    copies.append(pltpu.make_async_copy(q_ref, q_out, go.at[count]))
+    for copy in copies:
         copy.start()
-    for first, second in zip(into, out):
-        first.wait()
-        second.start()
-    for copy in out:
+    for copy in copies:
         copy.wait()
 
 
@@ -832,12 +859,13 @@
         pltpu.VMEM((RANK, LANES), F32),
         pltpu.VMEM((2, SIDE, SIDE, SHARE, LANES), F32),
         pltpu.VMEM((W, D), F32),
-        pltpu.VMEM((W, D), F32),
         pltpu.VMEM((2, HALF, LANES), F32),
         pltpu.VMEM((2, QB, LANES), F32),
         pltpu.VMEM((QB, LANES), F32),
         pltpu.VMEM((QB, LANES), F32),
-        pltpu.VMEM((ZLO - 1, QS, LANES), F32),
+        pltpu.VMEM((2, 3, QS, LANES), F32),
+        pltpu.VMEM((QS, LANES), F32),
+        pltpu.VMEM((QS, LANES), F32),
         pltpu.VMEM((2, QB, LANES), F32),
     ]
     counts = [12]
@@ -848,20 +876,16 @@
     counts += [1, 1, 1, 1, 1, 1]
     counts += [6, 6, 6, 6, 1, 1]
     counts += [1, 1, 2, 2]
-    counts += [1, 1, 1, 1, 1, 1, 1, 1]
-    counts += [1]
+    counts += [1, 1, 3, 3, 3, 3, 2, 2]
     flags = [pltpu.SemaphoreType.DMA((count,)) for count in counts]
     by_half = [
         array.reshape(PLANE, 2, ROWS, FFL) for array in (gate_pre, up_pre, hidden_grad)
     ]
     p_turned, q_turned = pl.pallas_call(
         kernel,
-        out_shape=(
-            jax.ShapeDtypeStruct((W, D), F32),
-            jax.ShapeDtypeStruct((W, FFL), F32),
-        ),
+        out_shape=(pltpu.VMEM((W, D), F32), pltpu.VMEM((W, FFL), F32)),
         in_specs=[vmem, vmem, far, far, far, vmem],
-        out_specs=(far, vmem),
+        out_specs=(vmem, vmem),
         scratch_shapes=buffers + flags,
         compiler_params=pltpu.CompilerParams(
             collective_id=0, has_side_effects=True, vmem_limit_bytes=56 * 2**20
@@ -875,17 +899,16 @@
     p_turned, q_turned = pl.pallas_call(
         deliver,
         out_shape=shapes,
-        in_specs=[far, far],
+        in_specs=[vmem, vmem],
         out_specs=(far, far),
         scratch_shapes=[
-            pltpu.VMEM((W, D), F32),
-            pltpu.VMEM((W, FFL), F32),
-            pltpu.SemaphoreType.DMA((7,)),
             pltpu.SemaphoreType.DMA((7,)),
         ],
-        compiler_params=pltpu.CompilerParams(vmem_limit_bytes=56 * 2**20),
         name="deliver",
-    )(p_turned, q_turned)
+    )(
+        pltpu.with_memory_space_constraint(p_turned, pltpu.VMEM),
+        pltpu.with_memory_space_constraint(q_turned, pltpu.VMEM),
+    )
     return p_turned.T, q_turned.T
 
 

time: 102 us -> 96.3 us (0.944)
  Pallas kernels: 102 us -> 95.5 us
    pallas_call x2, Pallas kernels: 102 us -> 95.5 us  [the longest x1 94.1 us: on_device(): pl.pallas_call(kernel, out_shape=(pltpu.VMEM((W, D), F32), pltpu.VMEM((W,...]
where the time goes in v4:
time: 96.3 us; the launch traced here: 96.1 us
  Pallas kernels  95.5 us (99%)
    pallas_call x1, Pallas kernels, on_device(): pl.pallas_call(kernel, out_shape=(pltpu.VMEM((W, D), F32), pltpu.VMEM((W,...  94.1 us

profile of v4, /device:TPU:1, one launch (start us, length us, event | category | flops | bytes accessed | tf_op | source)
XLA Modules:
  0.0 96.1 jit_solution(8887484077032721044)
XLA Ops:
  0.6 94.1 %power_step.1 = (f32[96,4608]{1,0:T(8,128)S(1)}, f32[96,1152]{1,0:T(8,128)S(1)}) custom-call(bf16[16,4608]{1,0:T(8,128)(2,1)} %in_ref.1, bf16[16,4608]{1,0:T(8,128)(2,1)} %og_ref.1, bf16[16,2,16,1152]{3,2,1,0:T(8,128)(2,1)} %bitcast.6, bf16[16,2,16,1152]{3,2,1,0:T(8,128)(2,1)} %bitcast.7, bf16[16,2,16,1152]{3,2,1,0:T(8,128)(2,1)} %bitcast.8, f32[96,1152]{1,0:T(8,128)} %bitcast.9), custom_call_target="tpu_custom_call" | custom-call | tf_op jit(solution)/shard_map/power_step/pallas_call | solution.py:884
  94.7 1.4 %deliver.1 = (f32[96,4608]{1,0:T(8,128)}, f32[96,1152]{1,0:T(8,128)}) custom-call(f32[96,4608]{1,0:T(8,128)S(1)} %get-tuple-element.6.p_ref, f32[96,1152]{1,0:T(8,128)S(1)} %get-tuple-element.7.q_ref), custom_call_target="tpu_custom_call" | custom-call | tf_op jit(solution)/shard_map/deliver/pallas_call | solution.py:899

commit v5 on v4

--- a/solution.py
+++ b/solution.py
@@ -244,12 +244,6 @@
 
     def far_first(count, body):
         if count == NEAR:
-
-            def step(i):
-                d = 1 + lax.rem(25 - i, 15)
-                body(d)
-                body(PLANE + d)
-
             body(jnp.int32(PLANE))
             around(15, lambda i: body(PLANE + 1 + lax.rem(25 - i, 15)), first=0)
             around(15, lambda i: body(1 + lax.rem(25 - i, 15)), first=0)
@@ -745,10 +739,20 @@
             qr_copy(d, far_chunk).start()
 
     q_own, q_across = q_rows(zl), q_rows(across)
-    drain(qr.at[1], qrr.at[1])
-    qx[...] = qh[q_across, :] + jnp.sum(qr[1], axis=0)
-    qx_copy = remote(qx, qy, qrs.at[2], qrr.at[2], zl_peer(across))
-    send_one(qx_copy)
+
+    def qx_copy(far):
+        return remote(
+            qx.at[far],
+            qy.at[1 - far],
+            qrs.at[2 + far],
+            qrr.at[3 - far],
+            zl_peer(across),
+        )
+
+    for far_chunk, rows in ((1, q_across), (0, q_own)):
+        drain(qr.at[far_chunk], qrr.at[far_chunk])
+        qx[far_chunk] = qh[rows, :] + jnp.sum(qr[far_chunk], axis=0)
+        qx_copy(far_chunk).start()
 
     gc_copy.wait_recv()
 
@@ -769,12 +773,6 @@
 
     finish()
 
-    drain(qr.at[0], qrr.at[0])
-    for far_chunk in range(2):
-        drain(qr.at[far_chunk], qrs.at[far_chunk])
-    qx_copy.wait_recv()
-    qf[core, q_own, :] = qh[q_own, :] + jnp.sum(qr[0], axis=0) + qy[...]
-
     def qg_copy(rows, kind, to):
         block = qf.at[core, rows]
         return remote(block, block, qgs.at[kind], qgr.at[kind], zl_peer(to))
@@ -786,19 +784,19 @@
         block = run_rows(start)
         return remote(block, block, qds.at[kind], qdr.at[kind], sibling)
 
-    qa_copy = qg_copy(q_own, 2, across)
-    send_one(qa_copy)
-    for d in (2, 3, 1):
-        qg_copy(q_own, 0, in_run(d)).start()
-    qa_copy.wait_recv()
-    for d in (2, 3, 1):
-        qg_copy(q_across, 1, in_run(d)).start()
+    for kind, rows in ((0, q_own), (1, q_across)):
+        qx_copy(1 - kind).wait_recv()
+        qf[core, rows, :] = qx[kind] + qy[kind]
+        for d in (2, 3, 1):
+            qg_copy(rows, kind, in_run(d)).start()
     run_bytes = qr.at[0]
     drain(run_bytes, qgr.at[0])
     send_one(qd_copy(run_start, 0))
     drain(run_bytes, qgr.at[1])
     send_one(qd_copy(4 - run_start, 1))
     for kind in range(2):
+        drain(run_bytes, qrs.at[kind])
+        qx_copy(kind).wait_send()
         drain(run_bytes, qgs.at[kind])
     for kind in range(2):
         qd_copy(run_start, kind).wait_recv()
@@ -864,8 +862,8 @@
         pltpu.VMEM((QB, LANES), F32),
         pltpu.VMEM((QB, LANES), F32),
         pltpu.VMEM((2, 3, QS, LANES), F32),
-        pltpu.VMEM((QS, LANES), F32),
-        pltpu.VMEM((QS, LANES), F32),
+        pltpu.VMEM((2, QS, LANES), F32),
+        pltpu.VMEM((2, QS, LANES), F32),
         pltpu.VMEM((2, QB, LANES), F32),
     ]
     counts = [12]
@@ -876,7 +874,7 @@
     counts += [1, 1, 1, 1, 1, 1]
     counts += [6, 6, 6, 6, 1, 1]
     counts += [1, 1, 2, 2]
-    counts += [1, 1, 3, 3, 3, 3, 2, 2]
+    counts += [1, 1, 4, 4, 2, 2, 2, 2]
     flags = [pltpu.SemaphoreType.DMA((count,)) for count in counts]
     by_half = [
         array.reshape(PLANE, 2, ROWS, FFL) for array in (gate_pre, up_pre, hidden_grad)

time: 96.3 us -> 94 us (0.976)
  Pallas kernels: 95.5 us -> 93.2 us
    pallas_call x1, Pallas kernels: 94.1 us -> 91.8 us  [on_device(): pl.pallas_call(kernel, out_shape=(pltpu.VMEM((W, D), F32), pltpu.VMEM((W,...]
where the time goes in v5:
time: 94 us; the launch traced here: 93.9 us
  Pallas kernels  93.2 us (99%)
    pallas_call x1, Pallas kernels, on_device(): pl.pallas_call(kernel, out_shape=(pltpu.VMEM((W, D), F32), pltpu.VMEM((W,...  91.8 us

profile of v5, /device:TPU:1, one launch (start us, length us, event | category | flops | bytes accessed | tf_op | source)
XLA Modules:
  0.0 93.9 jit_solution(16218385756901313325)
XLA Ops:
  0.6 91.8 %power_step.1 = (f32[96,4608]{1,0:T(8,128)S(1)}, f32[96,1152]{1,0:T(8,128)S(1)}) custom-call(bf16[16,4608]{1,0:T(8,128)(2,1)} %in_ref.1, bf16[16,4608]{1,0:T(8,128)(2,1)} %og_ref.1, bf16[16,2,16,1152]{3,2,1,0:T(8,128)(2,1)} %bitcast.6, bf16[16,2,16,1152]{3,2,1,0:T(8,128)(2,1)} %bitcast.7, bf16[16,2,16,1152]{3,2,1,0:T(8,128)(2,1)} %bitcast.8, f32[96,1152]{1,0:T(8,128)} %bitcast.9), custom_call_target="tpu_custom_call" | custom-call | tf_op jit(solution)/shard_map/power_step/pallas_call | solution.py:882
  92.4 1.4 %deliver.1 = (f32[96,4608]{1,0:T(8,128)}, f32[96,1152]{1,0:T(8,128)}) custom-call(f32[96,4608]{1,0:T(8,128)S(1)} %get-tuple-element.6.p_ref, f32[96,1152]{1,0:T(8,128)S(1)} %get-tuple-element.7.q_ref), custom_call_target="tpu_custom_call" | custom-call | tf_op jit(solution)/shard_map/deliver/pallas_call | solution.py:897

commit v6 on v5

--- a/solution.py
+++ b/solution.py
@@ -578,9 +578,7 @@
             send_one(g2_copy(portion, d))
 
 
-    quads = mm_t(zs[...], zs[...])
-    gram = quads[0:LANES, 0:LANES] + quads[LANES:, 0:LANES]
-    gram = gram + (quads[0:LANES, LANES:] + quads[LANES:, LANES:])
+    gram = mm_t(zb[...], zb[...], HIGH)
     row_at = lax.broadcasted_iota(jnp.int32, (RANK, LANES), 0)
     lane_at = lax.broadcasted_iota(jnp.int32, (RANK, LANES), 1)
     beside = jnp.zeros((RANK, LANES), F32)

time: 94 us -> 93.7 us (level)
  no operation moved by 1% of the time
where the time goes in v6:
time: 93.7 us; the launch traced here: 93.6 us
  Pallas kernels  93 us (99%)
    pallas_call x1, Pallas kernels, on_device(): pl.pallas_call(kernel, out_shape=(pltpu.VMEM((W, D), F32), pltpu.VMEM((W,...  91.5 us

profile of v6, /device:TPU:1, one launch (start us, length us, event | category | flops | bytes accessed | tf_op | source)
XLA Modules:
  0.0 93.6 jit_solution(11946715684448999061)
XLA Ops:
  0.6 91.5 %power_step.1 = (f32[96,4608]{1,0:T(8,128)S(1)}, f32[96,1152]{1,0:T(8,128)S(1)}) custom-call(bf16[16,4608]{1,0:T(8,128)(2,1)} %in_ref.1, bf16[16,4608]{1,0:T(8,128)(2,1)} %og_ref.1, bf16[16,2,16,1152]{3,2,1,0:T(8,128)(2,1)} %bitcast.6, bf16[16,2,16,1152]{3,2,1,0:T(8,128)(2,1)} %bitcast.7, bf16[16,2,16,1152]{3,2,1,0:T(8,128)(2,1)} %bitcast.8, f32[96,1152]{1,0:T(8,128)} %bitcast.9), custom_call_target="tpu_custom_call" | custom-call | tf_op jit(solution)/shard_map/power_step/pallas_call | solution.py:880
  92.2 1.4 %deliver.1 = (f32[96,4608]{1,0:T(8,128)}, f32[96,1152]{1,0:T(8,128)}) custom-call(f32[96,4608]{1,0:T(8,128)S(1)} %get-tuple-element.6.p_ref, f32[96,1152]{1,0:T(8,128)S(1)} %get-tuple-element.7.q_ref), custom_call_target="tpu_custom_call" | custom-call | tf_op jit(solution)/shard_map/deliver/pallas_call | solution.py:895

commit v7 on v6

--- a/solution.py
+++ b/solution.py
@@ -573,10 +573,6 @@
         to = lax.rem(side(portion) + d, SIDE)
         return remote(block, block, g1s.at[at], g1r.at[at], side_peer(portion, to))
 
-    for portion in range(2):
-        for d in (2, 1, 3):
-            send_one(g2_copy(portion, d))
-
 
     gram = mm_t(zb[...], zb[...], HIGH)
     row_at = lax.broadcasted_iota(jnp.int32, (RANK, LANES), 0)
@@ -604,6 +600,10 @@
     far_first(PLANE, lambda d: gp_copy(d).start())
     gp_bytes = gall.at[pl.ds(0, PLANE - 1)]
     pending.append(lambda: drain(gp_bytes, gps.at[0]))
+
+    for portion in range(2):
+        for d in (2, 1, 3):
+            send_one(g2_copy(portion, d))
 
     drain(urecv, ur.at[0])
     img[1, plane_rows, :] = ub[0] + jnp.sum(urecv[...], axis=0)

time: 93.7 us -> 95.6 us (1.020)
  Pallas kernels: 93 us -> 94.8 us
    pallas_call x1, Pallas kernels: 91.5 us -> 93.4 us  [on_device(): pl.pallas_call(kernel, out_shape=(pltpu.VMEM((W, D), F32), pltpu.VMEM((W,...]
where the time goes in v7:
time: 95.6 us; the launch traced here: 95.4 us
  Pallas kernels  94.8 us (99%)
    pallas_call x1, Pallas kernels, on_device(): pl.pallas_call(kernel, out_shape=(pltpu.VMEM((W, D), F32), pltpu.VMEM((W,...  93.4 us

profile of v7, /device:TPU:1, one launch (start us, length us, event | category | flops | bytes accessed | tf_op | source)
XLA Modules:
  0.0 95.4 jit_solution(12043931146771289864)
XLA Ops:
  0.6 93.4 %power_step.1 = (f32[96,4608]{1,0:T(8,128)S(1)}, f32[96,1152]{1,0:T(8,128)S(1)}) custom-call(bf16[16,4608]{1,0:T(8,128)(2,1)} %in_ref.1, bf16[16,4608]{1,0:T(8,128)(2,1)} %og_ref.1, bf16[16,2,16,1152]{3,2,1,0:T(8,128)(2,1)} %bitcast.6, bf16[16,2,16,1152]{3,2,1,0:T(8,128)(2,1)} %bitcast.7, bf16[16,2,16,1152]{3,2,1,0:T(8,128)(2,1)} %bitcast.8, f32[96,1152]{1,0:T(8,128)} %bitcast.9), custom_call_target="tpu_custom_call" | custom-call | tf_op jit(solution)/shard_map/power_step/pallas_call | solution.py:880
  94.0 1.4 %deliver.1 = (f32[96,4608]{1,0:T(8,128)}, f32[96,1152]{1,0:T(8,128)}) custom-call(f32[96,4608]{1,0:T(8,128)S(1)} %get-tuple-element.6.p_ref, f32[96,1152]{1,0:T(8,128)S(1)} %get-tuple-element.7.q_ref), custom_call_target="tpu_custom_call" | custom-call | tf_op jit(solution)/shard_map/deliver/pallas_call | solution.py:895
